TPU v7x, 32 devices: a whole 2x2x4 slice. The times are simulated.
32 devices in a mesh: section: 2 (over x), dp: 4 (over y, core), tensor: 4 (over z).
Axes of the slice: x: 2, y: 2, z: 4, core: 2. Of those that a mesh axis runs over, the one named last changes fastest.
Arguments:
- images_in: bfloat16 [2, 3152, 1024], P(None, ('dp', 'tensor')), may hold values from -6 to 6
- cotangent: bfloat16 [2, 3152, 1024], P(None, ('dp', 'tensor')), may hold values from -6 to 6
- w_qkv: bfloat16 [2, 1024, 3, 1024], P('section', 'dp', None, 'tensor'), may hold values from -0.1875 to 0.1875
- w_out: bfloat16 [2, 1024, 1024], P('section', 'dp', 'tensor'), may hold values from -0.75 to 0.75
- w_up: bfloat16 [2, 1024, 4096], P('section', 'dp', 'tensor'), may hold values from -0.1875 to 0.1875
- w_down: bfloat16 [2, 1024, 4096], P('section', 'dp', 'tensor'), may hold values from -0.09375 to 0.09375
- norm_gains: bfloat16 [2, 2, 1024], P('section', None, ('dp', 'tensor')), may hold values from 0.5 to 1.5
- row_shifts: bfloat16 [2, 4, 1024], P('section', None, ('dp', 'tensor')), may hold values from -3 to 3
- head_bias: bfloat16 [2, 2, 16, 64], P('section', None, 'tensor', 'dp'), may hold values from -3 to 3
- unit_bias: bfloat16 [2, 16, 256], P('section', 'tensor', 'dp'), may hold values from -3 to 3
Outputs:
- layer_out: bfloat16 [2, 2, 3152, 1024], P('section', None, ('dp', 'tensor'))
- input_grads: bfloat16 [2, 2, 3152, 1024], P('section', None, ('dp', 'tensor'))
- grad_qkv: float32 [2, 1024, 3, 1024], P('section', 'dp', None, 'tensor')
- grad_out: float32 [2, 1024, 1024], P('section', 'dp', 'tensor')
- grad_up: float32 [2, 1024, 4096], P('section', 'dp', 'tensor')
- grad_down: float32 [2, 1024, 4096], P('section', 'dp', 'tensor')
- grad_gains: float32 [2, 2, 1024], P('section', None, ('dp', 'tensor'))
- grad_shifts: float32 [2, 4, 1024], P('section', None, ('dp', 'tensor'))
- grad_head_bias: float32 [2, 2, 16, 64], P('section', None, 'tensor', 'dp')
- grad_unit_bias: float32 [2, 16, 256], P('section', 'tensor', 'dp')
All inputs are finite; a program needn't handle non-finite values.
Results may differ from a plain program's by a relative error of at most 0.018.
Values may be sent and summed in bfloat16 or wider, within the bound.
A program may use at most 256 MiB of HBM per device.

v0:
```python
from functools import partial

import jax
import jax.numpy as jnp
from jax import lax
from jax.sharding import PartitionSpec as P

HD = 64
SEQ = 197


SCORE_SCALE = 0.125
NORM_EPS = 1e-06
ROWS_CONTRACT = (((0,), (0,)), ((), ()))
LAST_CONTRACT = (((1,), (1,)), ((), ()))


def passed_along(value, axis, by):
    devices = lax.axis_size(axis)
    pairs = [(i, i + by) for i in range(devices) if 0 <= i + by < devices]
    return lax.ppermute(value, axis, pairs)


def normalize(values, scales, offsets):
    average = jnp.mean(values, axis=-1, keepdims=True)
    centred = values - average
    spread = jnp.mean(centred * centred, axis=-1, keepdims=True)
    return centred * lax.rsqrt(spread + NORM_EPS) * scales + offsets


def fetch_weights(sources):
    qkv_src, out_src, up_src, down_src, head_src, unit_src = sources
    gathered = (
        lax.all_gather(qkv_src[0], "dp", axis=0, tiled=True),
        lax.all_gather(out_src[0], "dp", axis=0, tiled=True),
        lax.all_gather(up_src[0], "dp", axis=0, tiled=True),
        lax.all_gather(down_src[0], "dp", axis=0, tiled=True),
        lax.all_gather(head_src[0], "dp", axis=2, tiled=True),
        lax.all_gather(unit_src[0], "dp", axis=1, tiled=True),
    )
    qkv_full, out_full, up_full, down_full, head_full, unit_full = gathered
    return (
        qkv_full.reshape(qkv_full.shape[0], -1),
        out_full,
        up_full,
        down_full,
        head_full.reshape(2, -1).astype(jnp.float32),
        unit_full.reshape(-1).astype(jnp.float32),
    )


def spread_rows(local_rows):
    return lax.all_gather(local_rows, "tensor", axis=0, tiled=True)


def spread_grads(local_rows):
    return lax.all_gather(local_rows, "tensor", axis=0, tiled=True)


def collect_rows(left_rows, right_side, rows_local):

    def partial_term(row_start, row_count):
        return lax.dot_general(
            left_rows, right_side, LAST_CONTRACT, preferred_element_type=jnp.float32
        )

    return lax.psum_scatter(
        partial_term(jnp.int32(0), lax.axis_size("tensor") * rows_local).astype(jnp.bfloat16),
        "tensor",
        scatter_dimension=0,
        tiled=True,
    ).astype(jnp.float32)


def collect_grads(left_rows, right_side, rows_local):

    def partial_term(row_start, row_count):
        return lax.dot_general(
            left_rows, right_side, LAST_CONTRACT, preferred_element_type=jnp.float32
        )

    return lax.psum_scatter(
        partial_term(jnp.int32(0), lax.axis_size("tensor") * rows_local).astype(jnp.bfloat16),
        "tensor",
        scatter_dimension=0,
        tiled=True,
    ).astype(jnp.float32)


def attend_image(operands):
    queries, key_rows, value_rows = operands
    scores = (
        jnp.einsum("sha,tha->hst", queries, key_rows, preferred_element_type=jnp.float32)
        * SCORE_SCALE
    )
    highest = jnp.max(scores, axis=-1, keepdims=True)
    weights = jnp.exp(scores - highest)
    totals = jnp.sum(weights, axis=-1, keepdims=True)
    probabilities = (weights / totals).astype(jnp.bfloat16)
    mixed_image = jnp.einsum(
        "hst,tha->sha", probabilities, value_rows, preferred_element_type=jnp.float32
    )
    return (mixed_image.astype(jnp.bfloat16), highest[..., 0] + jnp.log(totals[..., 0]))


def attend_back(operands):
    queries, key_rows, value_rows, log_total, grad_mixed = operands
    scores = (
        jnp.einsum("sha,tha->hst", queries, key_rows, preferred_element_type=jnp.float32)
        * SCORE_SCALE
    )
    probabilities = jnp.exp(scores - log_total[..., None])
    grad_probs = jnp.einsum(
        "sha,tha->hst", grad_mixed, value_rows, preferred_element_type=jnp.float32
    )
    centre = jnp.sum(probabilities * grad_probs, axis=-1, keepdims=True)
    grad_scores = (probabilities * (grad_probs - centre)).astype(jnp.bfloat16)
    grad_queries = (
        jnp.einsum("hst,tha->sha", grad_scores, key_rows, preferred_element_type=jnp.float32)
        * SCORE_SCALE
    )
    grad_keys = (
        jnp.einsum("hst,sha->tha", grad_scores, queries, preferred_element_type=jnp.float32)
        * SCORE_SCALE
    )
    grad_values = jnp.einsum(
        "hst,sha->tha",
        probabilities.astype(jnp.bfloat16),
        grad_mixed,
        preferred_element_type=jnp.float32,
    )
    return (
        grad_queries.astype(jnp.bfloat16),
        grad_keys.astype(jnp.bfloat16),
        grad_values.astype(jnp.bfloat16),
    )


def forward_layer(inputs, weights, row_params):
    qkv_weight, out_weight, up_weight, down_weight, head_terms, unit_terms = weights
    gains, shifts = row_params
    rows_local = inputs.shape[0]
    resid = inputs.astype(jnp.float32)
    normed = normalize(resid, gains[0], shifts[0]).astype(jnp.bfloat16)
    normed_full = spread_rows(normed)
    rows_all = normed_full.shape[0]
    local_width = head_terms.shape[1]
    heads_local = local_width // HD
    projected = jnp.dot(normed_full, qkv_weight, preferred_element_type=jnp.float32).reshape(
        rows_all, 3, local_width
    )
    queries = (projected[:, 0] + head_terms[0]).astype(jnp.bfloat16)
    key_rows = projected[:, 1].astype(jnp.bfloat16)
    value_rows = (projected[:, 2] + head_terms[1]).astype(jnp.bfloat16)
    image_shape = (rows_all // SEQ, SEQ, heads_local, HD)
    mixed_images, log_total = lax.map(
        attend_image,
        (
            queries.reshape(image_shape),
            key_rows.reshape(image_shape),
            value_rows.reshape(image_shape),
        ),
    )
    mixed_rows = mixed_images.reshape(rows_all, local_width)
    middle = resid + collect_rows(mixed_rows, out_weight, rows_local) + shifts[1]
    normed_two = normalize(middle, gains[1], shifts[2]).astype(jnp.bfloat16)
    normed_two_full = spread_rows(normed_two)
    hidden_pre = (
        jnp.dot(normed_two_full, up_weight, preferred_element_type=jnp.float32) + unit_terms
    )
    hidden = jax.nn.gelu(hidden_pre, approximate=False).astype(jnp.bfloat16)
    outputs = middle + collect_rows(hidden, down_weight, rows_local) + shifts[3]
    kept_state = (
        inputs,
        normed_full,
        queries,
        key_rows,
        value_rows,
        log_total,
        mixed_rows,
        middle,
        normed_two_full,
        hidden_pre,
        hidden,
    )
    return (outputs, kept_state)


def backward_layer(grad_output, kept_state, weights, row_params):
    (
        inputs,
        normed_full,
        queries,
        key_rows,
        value_rows,
        log_total,
        mixed_rows,
        middle,
        normed_two_full,
        hidden_pre,
        hidden,
    ) = kept_state
    qkv_weight, out_weight, up_weight, down_weight, head_terms, unit_terms = weights
    gains, shifts = row_params
    rows_local = inputs.shape[0]
    rows_all = normed_full.shape[0]
    local_width = head_terms.shape[1]
    heads_local = local_width // HD
    grad_top = grad_output.astype(jnp.float32)
    grad_top_full = spread_grads(grad_output)
    grad_down = lax.dot_general(
        grad_top_full, hidden, ROWS_CONTRACT, preferred_element_type=jnp.float32
    )
    grad_hidden = jnp.dot(grad_top_full, down_weight, preferred_element_type=jnp.float32)
    gelu_value, gelu_back = jax.vjp(partial(jax.nn.gelu, approximate=False), hidden_pre)
    grad_pre = gelu_back(grad_hidden)[0].astype(jnp.bfloat16)
    grad_unit = jnp.sum(grad_pre.astype(jnp.float32), axis=0)
    grad_up = lax.dot_general(
        normed_two_full, grad_pre, ROWS_CONTRACT, preferred_element_type=jnp.float32
    )
    grad_normed_two = collect_grads(grad_pre, up_weight, rows_local)
    norm_value, norm_back_two = jax.vjp(normalize, middle, gains[1], shifts[2])
    grad_mid_norm, grad_gain_two, grad_shift_two = norm_back_two(grad_normed_two)
    grad_middle = grad_top + grad_mid_norm
    grad_branch_full = spread_grads(grad_middle.astype(jnp.bfloat16))
    grad_out_weight = lax.dot_general(
        grad_branch_full, mixed_rows, ROWS_CONTRACT, preferred_element_type=jnp.float32
    )
    grad_mixed = jnp.dot(grad_branch_full, out_weight, preferred_element_type=jnp.float32).astype(
        jnp.bfloat16
    )
    image_shape = (rows_all // SEQ, SEQ, heads_local, HD)
    grad_queries, grad_keys, grad_values = lax.map(
        attend_back,
        (
            queries.reshape(image_shape),
            key_rows.reshape(image_shape),
            value_rows.reshape(image_shape),
            log_total,
            grad_mixed.reshape(image_shape),
        ),
    )
    grad_queries = grad_queries.reshape(rows_all, local_width)
    grad_keys = grad_keys.reshape(rows_all, local_width)
    grad_values = grad_values.reshape(rows_all, local_width)
    grad_proj = jnp.stack([grad_queries, grad_keys, grad_values], axis=1).reshape(
        rows_all, 3 * local_width
    )
    grad_head = jnp.stack(
        [
            jnp.sum(grad_queries.astype(jnp.float32), axis=0),
            jnp.sum(grad_values.astype(jnp.float32), axis=0),
        ]
    )
    grad_qkv_weight = lax.dot_general(
        normed_full, grad_proj, ROWS_CONTRACT, preferred_element_type=jnp.float32
    )
    grad_normed = collect_grads(grad_proj, qkv_weight, rows_local)
    norm_first, norm_back_one = jax.vjp(normalize, inputs.astype(jnp.float32), gains[0], shifts[0])
    grad_in_norm, grad_gain_one, grad_shift_one = norm_back_one(grad_normed)
    grad_inputs = grad_middle + grad_in_norm
    row_grads = (
        jnp.stack([grad_gain_one, grad_gain_two]),
        jnp.stack(
            [
                grad_shift_one,
                jnp.sum(grad_middle, axis=0),
                grad_shift_two,
                jnp.sum(grad_top, axis=0),
            ]
        ),
    )
    weight_grads = (
        grad_qkv_weight.reshape(grad_qkv_weight.shape[0], 3, local_width),
        grad_out_weight,
        grad_up,
        grad_down,
        grad_head.reshape(2, heads_local, HD),
        grad_unit.reshape(heads_local, -1),
    )
    return (grad_inputs, weight_grads, row_grads)


def reduce_grads(weight_grads):
    return (
        lax.psum_scatter(
            weight_grads[0].astype(jnp.bfloat16), "dp", scatter_dimension=0, tiled=True
        ).astype(jnp.float32),
        lax.psum_scatter(
            weight_grads[1].astype(jnp.bfloat16), "dp", scatter_dimension=0, tiled=True
        ).astype(jnp.float32),
        lax.psum_scatter(
            weight_grads[2].astype(jnp.bfloat16), "dp", scatter_dimension=0, tiled=True
        ).astype(jnp.float32),
        lax.psum_scatter(
            weight_grads[3].astype(jnp.bfloat16), "dp", scatter_dimension=0, tiled=True
        ).astype(jnp.float32),
        lax.psum_scatter(
            weight_grads[4].astype(jnp.bfloat16), "dp", scatter_dimension=2, tiled=True
        ).astype(jnp.float32),
        lax.psum_scatter(
            weight_grads[5].astype(jnp.bfloat16), "dp", scatter_dimension=1, tiled=True
        ).astype(jnp.float32),
    )


def add_trees(first_tree, second_tree):
    if first_tree is None:
        return second_tree
    return jax.tree.map(jnp.add, first_tree, second_tree)


def pick_tree(flag_value, lower_tree, upper_tree):
    return jax.tree.map(
        lambda lower_leaf, upper_leaf: jnp.where(flag_value, lower_leaf, upper_leaf),
        lower_tree,
        upper_tree,
    )


def on_device(
    images_in, cotangent, w_qkv, w_out, w_up, w_down, norm_gains, row_shifts, head_bias, unit_bias
):
    is_first = lax.axis_index("section") == 0
    micro_count = images_in.shape[0]
    gathered_rows = (
        lax.all_gather(norm_gains[0], ("dp", "tensor"), axis=1, tiled=True),
        lax.all_gather(row_shifts[0], ("dp", "tensor"), axis=1, tiled=True),
    )
    row_params = (gathered_rows[0].astype(jnp.float32), gathered_rows[1].astype(jnp.float32))
    sources = (w_qkv, w_out, w_up, w_down, head_bias, unit_bias)
    zero_rows = jnp.zeros_like(images_in[0])
    received = zero_rows
    grad_received = zero_rows
    outputs_seen, grads_seen, kept_seen = ([], [], [])
    weight_total = None
    weight_shards = None
    row_total = None
    for moment in range(micro_count + 2):
        if moment <= micro_count:
            weights = fetch_weights(sources)
            source = images_in[min(moment, micro_count - 1)]
            if moment == 0:
                layer_input = source
            elif moment == micro_count:
                layer_input = received
            else:
                layer_input = jnp.where(is_first, source, received)
            outputs, kept_state = forward_layer(layer_input, weights, row_params)
            output_low = outputs.astype(jnp.bfloat16)
            outputs_seen.append(output_low)
            kept_seen.append(kept_state)
            if moment < micro_count:
                received = passed_along(output_low, "section", 1)
        if moment >= 1:
            weights = fetch_weights(sources)
            upper_grad = cotangent[moment - 1] if moment <= micro_count else zero_rows
            lower_grad = grad_received if moment >= 2 else zero_rows
            grad_output = jnp.where(is_first, lower_grad, upper_grad)
            kept_upper = kept_seen[moment] if moment <= micro_count else kept_seen[moment - 2]
            kept_lower = kept_seen[moment - 2] if moment >= 2 else kept_seen[moment]
            kept_state = pick_tree(is_first, kept_lower, kept_upper)
            grad_inputs, weight_grads, row_grads = backward_layer(
                grad_output, kept_state, weights, row_params
            )
            grad_low = grad_inputs.astype(jnp.bfloat16)
            grads_seen.append(grad_low)
            if moment <= micro_count:
                grad_received = passed_along(grad_low, "section", -1)
            row_total = add_trees(row_total, row_grads)
            weight_total = add_trees(weight_total, weight_grads)
    weight_shards = reduce_grads(weight_total)
    row_shards = lax.psum_scatter(row_total, ("dp", "tensor"), scatter_dimension=1, tiled=True)
    layer_out = jnp.stack(
        [
            jnp.where(is_first, outputs_seen[slot_index], outputs_seen[slot_index + 1])
            for slot_index in range(micro_count)
        ]
    )[None]
    input_grads = jnp.stack(
        [
            jnp.where(is_first, grads_seen[slot_index + 1], grads_seen[slot_index])
            for slot_index in range(micro_count)
        ]
    )[None]
    return (
        layer_out,
        input_grads,
        weight_shards[0][None],
        weight_shards[1][None],
        weight_shards[2][None],
        weight_shards[3][None],
        row_shards[0][None],
        row_shards[1][None],
        weight_shards[4][None],
        weight_shards[5][None],
    )


def solution(mesh):
    in_specs = (
        P(None, ("dp", "tensor"), None),
        P(None, ("dp", "tensor"), None),
        P("section", "dp", None, "tensor"),
        P("section", "dp", "tensor"),
        P("section", "dp", "tensor"),
        P("section", "dp", "tensor"),
        P("section", None, ("dp", "tensor")),
        P("section", None, ("dp", "tensor")),
        P("section", None, "tensor", "dp"),
        P("section", "tensor", "dp"),
    )
    out_specs = (
        P("section", None, ("dp", "tensor"), None),
        P("section", None, ("dp", "tensor"), None),
        P("section", "dp", None, "tensor"),
        P("section", "dp", "tensor"),
        P("section", "dp", "tensor"),
        P("section", "dp", "tensor"),
        P("section", None, ("dp", "tensor")),
        P("section", None, ("dp", "tensor")),
        P("section", None, "tensor", "dp"),
        P("section", "tensor", "dp"),
    )
    return jax.shard_map(
        on_device, mesh=mesh, in_specs=in_specs, out_specs=out_specs, check_vma=False
    )
```

profile of v0, /device:TPU:21, one launch (start us, length us, event | category | flops | bytes accessed | tf_op | source)
XLA Modules:
  0.0 1726.1 jit_solution(18410249713080127118)
XLA Ops:
  8.7 31.0 %all-gather = bf16[1,2,1024]{1,0,2:T(2,128)(2,1)S(1)} all-gather(bf16[1,2,64]{1,0,2:T(2,128)(2,1)S(1)} %copy.328), channel_id=2, replica_groups=mesh['section'=2,'dp'=4,'tensor'=4] {'dp','tensor'}, dimensions={2}, use_global_device_ids=true | all-gather | bytes 4352 | tf_op jit(solution)/shard_map/all_gather | solution.py:327
  41.1 36.1 %all-gather.1 = bf16[1,4,1024]{1,0,2:T(2,128)(2,1)S(1)} all-gather(bf16[1,4,64]{1,0,2:T(2,128)(2,1)S(1)} %copy.329), channel_id=3, replica_groups=mesh['section'=2,'dp'=4,'tensor'=4] {'dp','tensor'}, dimensions={2}, use_global_device_ids=true | all-gather | bytes 8704 | tf_op jit(solution)/shard_map/all_gather | solution.py:328
  80.2 7.2 slice_reduce_fusion.5
  87.4 21.9 %slice_reduce_fusion = (f32[1024]{0:T(1024)S(1)}, f32[1024]{0:T(1024)S(1)}, f32[1024]{0:T(1024)S(1)}, f32[1024]{0:T(1024)S(1)}) fusion(f32[1,4,1024]{1,0,2:T(1,128)S(1)} %convert_element_type.485), kind=kLoop, calls=%fused_computation.445 | loop fusion | bytes 32768 | tf_op jit(solution)/shard_map/slice | solution.py:172
  116.0 7.7 all-gather.4
  126.6 23.7 %all-gather.44.cloned.1.call-done = bf16[4,197,1024]{2,1,0:T(8,128)(2,1)} async-done(((bf16[1,197,1024]{2,1,0:T(8,128)(2,1)}), bf16[4,197,1024]{2,1,0:T(8,128)(2,1)}) %all-gather.44.cloned.1.call-update) | async-done | bytes 1613840 | tf_op jit(solution)/shard_map/all_gather | solution.py:53
  168.4 13.4 while.78
  185.5 31.7 %fusion = bf16[200,1024]{1,0:T(8,128)(2,1)S(1)} fusion(bf16[788,1024]{1,0:T(8,128)(2,1)} %convolution_convert_fusion.8), kind=kCustom, calls=%all-reduce-scatter | all-reduce-scatter fusion | flops 819201 | bytes 2023936
  225.7 8.1 all-gather.6
  233.9 30.1 %all-gather.46.cloned.1.call-done = bf16[4,197,1024]{2,1,0:T(8,128)(2,1)} async-done(((bf16[1,197,1024]{2,1,0:T(8,128)(2,1)}), bf16[4,197,1024]{2,1,0:T(8,128)(2,1)}) %all-gather.46.cloned.1.call-update) | async-done | bytes 1613840 | tf_op jit(solution)/shard_map/all_gather | solution.py:53
  267.0 20.5 %all-gather.38.cloned.1.call-done = bf16[1,1024,1024]{2,1,0:T(8,128)(2,1)} async-done(((bf16[1,256,1024]{2,1,0:T(8,128)(2,1)}), bf16[1,1024,1024]{2,1,0:T(8,128)(2,1)}) %all-gather.38.cloned.1.call-update) | async-done | bytes 2097168 | tf_op jit(solution)/shard_map/all_gather | solution.py:36
  287.5 12.2 fusion.140
  299.7 11.8 all-gather.40.cloned.1.call-done
  316.7 31.8 %fusion.1 = bf16[200,1024]{1,0:T(8,128)(2,1)S(1)} fusion(bf16[788,1024]{1,0:T(8,128)(2,1)} %fusion.214), kind=kCustom, calls=%all-reduce-scatter.1 | all-reduce-scatter fusion | flops 819201 | bytes 2023936
  364.9 41.4 %all-gather.48.cloned.1.call-done = bf16[4,197,1024]{2,1,0:T(8,128)(2,1)} async-done(((bf16[1,197,1024]{2,1,0:T(8,128)(2,1)}), bf16[4,197,1024]{2,1,0:T(8,128)(2,1)}) %all-gather.48.cloned.1.call-update) | async-done | bytes 1613840 | tf_op jit(solution)/shard_map/all_gather | solution.py:53
  428.9 9.4 while.79
  445.8 31.6 %fusion.2 = bf16[200,1024]{1,0:T(8,128)(2,1)S(1)} fusion(bf16[788,1024]{1,0:T(8,128)(2,1)} %convolution_convert_fusion.7), kind=kCustom, calls=%all-reduce-scatter.2 | all-reduce-scatter fusion | flops 819201 | bytes 2023936
  491.5 32.6 %all-gather.50.cloned.1.call-done = bf16[4,197,1024]{2,1,0:T(8,128)(2,1)} async-done(((bf16[1,197,1024]{2,1,0:T(8,128)(2,1)}), bf16[4,197,1024]{2,1,0:T(8,128)(2,1)}) %all-gather.50.cloned.1.call-update) | async-done | bytes 1613840 | tf_op jit(solution)/shard_map/all_gather | solution.py:53
  527.1 12.1 multiply_convert_fusion.3
  543.4 69.5 %fusion.3 = bf16[200,1024]{1,0:T(8,128)(2,1)S(1)} fusion(bf16[788,1024]{1,0:T(8,128)(2,1)} %fusion.217), kind=kCustom, calls=%all-reduce-scatter.3 | all-reduce-scatter fusion | flops 819201 | bytes 2023936
  626.3 7.3 collective-permute-done.1
  635.5 8.1 convert_reduce_fusion.2
  647.8 27.1 %all-gather.52.cloned.1.call-done = bf16[4,197,1024]{2,1,0:T(8,128)(2,1)} async-done(((bf16[1,197,1024]{2,1,0:T(8,128)(2,1)}), bf16[4,197,1024]{2,1,0:T(8,128)(2,1)}) %all-gather.52.cloned.1.call-update) | async-done | bytes 1613840 | tf_op jit(solution)/shard_map/all_gather | solution.py:53
  708.5 13.3 while.80
  729.3 58.0 %fusion.347 = (bf16[200,1024]{1,0:T(8,128)(2,1)}, bf16[200,1024]{1,0:T(8,128)(2,1)}) fusion(bf16[788,1024]{1,0:T(8,128)(2,1)} %fusion.205, bf16[788,1024]{1,0:T(8,128)(2,1)} %convolution_convert_fusion.6), kind=kCustom, calls=%all-reduce-scatter.13 | all-reduce-scatter fusion | flops 1638401 | bytes 4047360
  811.6 36.1 %all-gather.56.cloned.1.call-done = bf16[4,197,1024]{2,1,0:T(8,128)(2,1)} async-done(((bf16[1,197,1024]{2,1,0:T(8,128)(2,1)}), bf16[4,197,1024]{2,1,0:T(8,128)(2,1)}) %all-gather.56.cloned.1.call-update) | async-done | bytes 1613840 | tf_op jit(solution)/shard_map/all_gather | solution.py:57
  858.1 17.9 %while.81 = (s32[]{:T(128)}, bf16[4,197,4,64]{1,3,2,0:T(8,128)(2,1)}, bf16[4,197,4,64]{1,3,2,0:T(8,128)(2,1)}, bf16[4,197,4,64]{1,3,2,0:T(8,128)(2,1)}, bf16[4,1...) while((s32[]{:T(128)}, ...), condition=%wide.region_35.36_spmd, body=%wide.region_33.35_spmd.sunk | while | flops 100844304 | bytes 6584497 | solution.py:233
  894.2 31.5 %fusion.7 = bf16[200,1024]{1,0:T(8,128)(2,1)S(1)} fusion(bf16[788,1024]{1,0:T(8,128)(2,1)} %bitcast_convert_fusion.2), kind=kCustom, calls=%all-reduce-scatter.7 | all-reduce-scatter fusion | flops 819201 | bytes 2023936
  942.3 8.7 collective-permute-done.2
  955.5 11.7 fusion.144
  967.2 24.3 %all-gather.58.cloned.1.call-done = bf16[4,197,1024]{2,1,0:T(8,128)(2,1)} async-done(((bf16[1,197,1024]{2,1,0:T(8,128)(2,1)}), bf16[4,197,1024]{2,1,0:T(8,128)(2,1)}) %all-gather.58.cloned.1.call-update) | async-done | bytes 1613840 | tf_op jit(solution)/shard_map/all_gather | solution.py:57
  994.6 12.8 convert_reduce_fusion.1
  1011.6 32.6 %fusion.8 = bf16[200,1024]{1,0:T(8,128)(2,1)} fusion(bf16[788,1024]{1,0:T(8,128)(2,1)} %fusion.208), kind=kCustom, calls=%all-reduce-scatter.8 | all-reduce-scatter fusion | flops 819201 | bytes 2023936
  1065.3 33.7 %all-gather.60.cloned.1.call-done = bf16[4,197,1024]{2,1,0:T(8,128)(2,1)} async-done(((bf16[1,197,1024]{2,1,0:T(8,128)(2,1)}), bf16[4,197,1024]{2,1,0:T(8,128)(2,1)}) %all-gather.60.cloned.1.call-update) | async-done | bytes 1613840 | tf_op jit(solution)/shard_map/all_gather | solution.py:57
  1109.4 29.0 %while.82 = (s32[]{:T(128)}, bf16[4,197,4,64]{1,3,2,0:T(8,128)(2,1)}, bf16[4,197,4,64]{1,3,2,0:T(8,128)(2,1)}, bf16[4,197,4,64]{1,3,2,0:T(8,128)(2,1)}, bf16[4,1...) while((s32[]{:T(128)}, ...), condition=%wide.region_46.47_spmd, body=%wide.region_44.46_spmd.sunk | while | flops 100844304 | bytes 6187041 | solution.py:233
  1156.5 32.4 %fusion.9 = bf16[200,1024]{1,0:T(8,128)(2,1)} fusion(bf16[788,1024]{1,0:T(8,128)(2,1)} %bitcast_convert_fusion.1), kind=kCustom, calls=%all-reduce-scatter.9 | all-reduce-scatter fusion | flops 819201 | bytes 2023936
  1206.0 8.7 collective-permute-done.3
  1215.8 39.3 %all-gather.62.cloned.1.call-done = bf16[4,197,1024]{2,1,0:T(8,128)(2,1)} async-done(((bf16[1,197,1024]{2,1,0:T(8,128)(2,1)}), bf16[4,197,1024]{2,1,0:T(8,128)(2,1)}) %all-gather.62.cloned.1.call-update) | async-done | bytes 1613840 | tf_op jit(solution)/shard_map/all_gather | solution.py:57
  1269.5 31.6 %fusion.10 = bf16[200,1024]{1,0:T(8,128)(2,1)S(1)} fusion(bf16[788,1024]{1,0:T(8,128)(2,1)} %fusion.211), kind=kCustom, calls=%all-reduce-scatter.10 | all-reduce-scatter fusion | flops 819201 | bytes 2023936
  1329.7 22.7 %all-gather.64.cloned.1.call-done = bf16[4,197,1024]{2,1,0:T(8,128)(2,1)} async-done(((bf16[1,197,1024]{2,1,0:T(8,128)(2,1)}), bf16[4,197,1024]{2,1,0:T(8,128)(2,1)}) %all-gather.64.cloned.1.call-update) | async-done | bytes 1613840 | tf_op jit(solution)/shard_map/all_gather | solution.py:57
  1362.7 17.9 %while.83 = (s32[]{:T(128)}, bf16[4,197,4,64]{1,3,2,0:T(8,128)(2,1)}, bf16[4,197,4,64]{1,3,2,0:T(8,128)(2,1)}, bf16[4,197,4,64]{1,3,2,0:T(8,128)(2,1)}, bf16[4,1...) while((s32[]{:T(128)}, ...), condition=%wide.region_57.58_spmd, body=%wide.region_55.57_spmd.sunk | while | flops 100844304 | bytes 6584497 | solution.py:233
  1395.1 57.8 %fusion.346 = (bf16[200,1024]{1,0:T(8,128)(2,1)}, bf16[200,1024]{1,0:T(8,128)(2,1)S(1)}) fusion(bf16[788,1024]{1,0:T(8,128)(2,1)} %fusion.220, bf16[788,1024]{1,0:T(8,128)(2,1)} %bitcast_convert_fusion), kind=kCustom, calls=%all-reduce-scatter.12 | all-reduce-scatter fusion | flops 1638401 | bytes 4047360
  1517.6 16.3 reduce-scatter.49.cloned.1.call-done
  1535.4 57.4 %reduce-scatter.51.cloned.1.call-done = f32[64,4]{1,0:T(8,128)} async-done(((f32[1024,4]{1,0:T(8,128)}), f32[64,4]{1,0:T(8,128)}) %reduce-scatter.51.cloned.1.call-update) | async-done | bytes 1040
  1594.2 24.2 %reduce-scatter.43.cloned.1.call-done = bf16[256,256]{1,0:T(8,128)(2,1)} async-done(((bf16[1024,256]{1,0:T(8,128)(2,1)}), bf16[256,256]{1,0:T(8,128)(2,1)}) %reduce-scatter.43.cloned.1.call-update) | async-done | bytes 131088 | tf_op jit(solution)/shard_map/reduce_scatter | solution.py:289
  1620.0 32.5 %reduce-scatter.47.cloned.1.call-done = bf16[256,1024]{1,0:T(8,128)(2,1)} async-done(((bf16[1024,1024]{1,0:T(8,128)(2,1)}), bf16[256,1024]{1,0:T(8,128)(2,1)}) %reduce-scatter.47.cloned.1.call-update) | async-done | bytes 524304 | tf_op jit(solution)/shard_map/reduce_scatter | solution.py:295
  1654.6 31.9 %reduce-scatter.45.cloned.1.call-done = bf16[256,1024]{1,0:T(8,128)(2,1)} async-done(((bf16[1024,1024]{1,0:T(8,128)(2,1)}), bf16[256,1024]{1,0:T(8,128)(2,1)}) %reduce-scatter.45.cloned.1.call-update) | async-done | bytes 524304 | tf_op jit(solution)/shard_map/reduce_scatter | solution.py:292
  1688.6 28.8 %reduce-scatter.41.cloned.1.call-done = bf16[256,3,256]{2,0,1:T(8,128)(2,1)} async-done(((bf16[1024,3,256]{2,0,1:T(8,128)(2,1)}), bf16[256,3,256]{2,0,1:T(8,128)(2,1)}) %reduce-scatter.41.cloned.1.call-update) | async-done | bytes 393232 | tf_op jit(solution)/shard_map/reduce_scatter | solution.py:286
  (680 shorter events, 572.6 us)
Async XLA Ops:
  7.2 70.5 %copy-start.26 = (bf16[2,197,1024]{2,0,1:T(2,128)(2,1)S(1)}, bf16[2,197,1024]{2,0,1:T(2,128)(2,1)}, u32[]{:S(2)}) copy-start(bf16[2,197,1024]{2,0,1:T(2,128)(2,1)} %param.22) | copy-start | bytes 2420740
  7.2 116.6 %all-gather.36.cloned.1.call-start = ((), (), s32[]{:S(2)}) async-start(), calls=%async_computation.12 | async-start | bytes 1966080 | tf_op jit(solution)/shard_map/all_gather | solution.py:34
  7.9 142.3 %all-gather.44.cloned.1.call-start = ((), (), s32[]{:S(2)}) async-start(), calls=%async_computation.16 | async-start | bytes 2048000 | tf_op jit(solution)/shard_map/all_gather | solution.py:53
  109.3 511.7 %copy-start.53 = (f32[1024]{0:T(1024)}, f32[1024]{0:T(1024)S(1)}, u32[]{:S(2)}) copy-start(f32[1024]{0:T(1024)S(1)} %get-tuple-element.558) | copy-start | bytes 12292
  110.4 153.6 %all-gather.46.cloned.1.call-start = ((), (), s32[]{:S(2)}) async-start(), calls=%async_computation.17 | async-start | bytes 2048000 | tf_op jit(solution)/shard_map/all_gather | solution.py:53
  217.3 4.7 collective-permute-start.4
  224.4 63.1 %all-gather.38.cloned.1.call-start = ((), (), s32[]{:S(2)}) async-start(), calls=%async_computation.13 | async-start | bytes 2621440 | tf_op jit(solution)/shard_map/all_gather | solution.py:36
  225.0 86.6 %all-gather.40.cloned.1.call-start = ((), (), s32[]{:S(2)}) async-start(), calls=%async_computation.14 | async-start | bytes 2621440 | tf_op jit(solution)/shard_map/all_gather | solution.py:37
  225.6 180.7 %all-gather.48.cloned.1.call-start = ((), (), s32[]{:S(2)}) async-start(), calls=%async_computation.18 | async-start | bytes 2048000 | tf_op jit(solution)/shard_map/all_gather | solution.py:53
  348.5 4.7 collective-permute-start.5
  354.2 8.9 collective-permute-start
  364.7 159.4 %all-gather.50.cloned.1.call-start = ((), (), s32[]{:S(2)}) async-start(), calls=%async_computation.19 | async-start | bytes 2048000 | tf_op jit(solution)/shard_map/all_gather | solution.py:53
  477.4 4.7 collective-permute-start.6
  484.5 151.0 %all-gather.42.cloned.1.call-start = ((), (), s32[]{:S(2)}) async-start(), calls=%async_computation.15 | async-start | bytes 4034560 | tf_op jit(solution)/shard_map/all_gather | solution.py:57
  491.3 183.6 %all-gather.52.cloned.1.call-start = ((), (), s32[]{:S(2)}) async-start(), calls=%async_computation.20 | async-start | bytes 2048000 | tf_op jit(solution)/shard_map/all_gather | solution.py:53
  612.9 4.7 collective-permute-start.7
  623.3 10.3 collective-permute-start.1
  633.6 175.2 %copy-start = (bf16[197,1024]{1,0:T(8,128)(2,1)}, bf16[197,1024]{1,0:T(8,128)(2,1)S(1)}, u32[]{:S(2)}) copy-start(bf16[197,1024]{1,0:T(8,128)(2,1)S(1)} %collective-permute-done.1) | copy-start | bytes 1210372
  635.0 212.7 %all-gather.56.cloned.1.call-start = ((), (), s32[]{:S(2)}) async-start(), calls=%async_computation.22 | async-start | bytes 2048000 | tf_op jit(solution)/shard_map/all_gather | solution.py:57
  788.0 5.3 collective-permute-start.10
  791.4 5.8 collective-permute-start.8
  808.7 143.7 %all-gather.54.cloned.1.call-start = ((), (), s32[]{:S(2)}) async-start(), calls=%async_computation.21 | async-start | bytes 2048000 | tf_op jit(solution)/shard_map/all_gather | solution.py:53
  811.6 179.9 %all-gather.58.cloned.1.call-start = ((), (), s32[]{:S(2)}) async-start(), calls=%async_computation.23 | async-start | bytes 2048000 | tf_op jit(solution)/shard_map/all_gather | solution.py:57
  926.5 4.8 collective-permute-start.11
  941.0 10.0 collective-permute-start.2
  951.9 147.1 %all-gather.60.cloned.1.call-start = ((), (), s32[]{:S(2)}) async-start(), calls=%async_computation.24 | async-start | bytes 2048000 | tf_op jit(solution)/shard_map/all_gather | solution.py:57
  1045.0 4.7 collective-permute-start.12
  1059.5 195.7 %all-gather.62.cloned.1.call-start = ((), (), s32[]{:S(2)}) async-start(), calls=%async_computation.25 | async-start | bytes 2048000 | tf_op jit(solution)/shard_map/all_gather | solution.py:57
  1189.7 4.7 collective-permute-start.13
  1204.7 10.0 collective-permute-start.3
  1215.6 136.8 %all-gather.64.cloned.1.call-start = ((), (), s32[]{:S(2)}) async-start(), calls=%async_computation.26 | async-start | bytes 2048000 | tf_op jit(solution)/shard_map/all_gather | solution.py:57
  1301.1 4.7 collective-permute-start.14
  1312.9 189.4 %reduce-scatter.55.cloned.1.call-start = ((), (), s32[]{:S(2)}) async-start(), calls=%async_computation.30 | async-start | bytes 81920
  1329.5 176.7 %reduce-scatter.53.cloned.1.call-start = ((), (), s32[]{:S(2)}) async-start(), calls=%async_computation.29 | async-start | bytes 20480
  1395.1 67.4 %copy-start.59 = (f32[1024]{0:T(1024)S(1)}, f32[1024]{0:T(1024)}, u32[]{:S(2)}) copy-start(f32[1024]{0:T(1024)} %get-tuple-element.679) | copy-start | bytes 12292
  1395.1 67.4 %copy-start.60 = (f32[1024]{0:T(1024)S(1)}, f32[1024]{0:T(1024)}, u32[]{:S(2)}) copy-start(f32[1024]{0:T(1024)} %get-tuple-element.569) | copy-start | bytes 12292
  1395.1 67.4 %copy-start.61 = (f32[1024]{0:T(1024)S(1)}, f32[1024]{0:T(1024)}, u32[]{:S(2)}) copy-start(f32[1024]{0:T(1024)} %get-tuple-element.677) | copy-start | bytes 12292
  1395.1 67.4 %copy-start.62 = (f32[1024]{0:T(1024)S(1)}, f32[1024]{0:T(1024)}, u32[]{:S(2)}) copy-start(f32[1024]{0:T(1024)} %get-tuple-element.573) | copy-start | bytes 12292
  1395.1 67.4 %copy-start.63 = (f32[1024]{0:T(1024)S(1)}, f32[1024]{0:T(1024)}, u32[]{:S(2)}) copy-start(f32[1024]{0:T(1024)} %get-tuple-element.566) | copy-start | bytes 12292
  1395.1 67.4 %copy-start.64 = (f32[1024]{0:T(1024)S(1)}, f32[1024]{0:T(1024)}, u32[]{:S(2)}) copy-start(f32[1024]{0:T(1024)} %get-tuple-element.565) | copy-start | bytes 12292
  1453.0 4.8 collective-permute-start.15
  1456.3 77.7 %reduce-scatter.49.cloned.1.call-start = ((), (), s32[]{:S(2)}) async-start(), calls=%async_computation.27 | async-start | bytes 557056
  1462.4 130.3 %reduce-scatter.51.cloned.1.call-start = ((), (), s32[]{:S(2)}) async-start(), calls=%async_computation.28 | async-start | bytes 557056
  1463.7 154.7 %reduce-scatter.43.cloned.1.call-start = ((), (), s32[]{:S(2)}) async-start(), calls=%async_computation.9 | async-start | bytes 655360 | tf_op jit(solution)/shard_map/reduce_scatter | solution.py:289
  1466.8 185.7 %reduce-scatter.47.cloned.1.call-start = ((), (), s32[]{:S(2)}) async-start(), calls=%async_computation.11 | async-start | bytes 2621440 | tf_op jit(solution)/shard_map/reduce_scatter | solution.py:295
  1475.6 210.9 %reduce-scatter.45.cloned.1.call-start = ((), (), s32[]{:S(2)}) async-start(), calls=%async_computation.10 | async-start | bytes 2621440 | tf_op jit(solution)/shard_map/reduce_scatter | solution.py:292
  1486.4 231.0 %reduce-scatter.41.cloned.1.call-start = ((), (), s32[]{:S(2)}) async-start(), calls=%async_computation.8 | async-start | bytes 1966080 | tf_op jit(solution)/shard_map/reduce_scatter | solution.py:286
  1503.8 4.7 collective-permute-start.9
  (85 other events, 1430.7 us)
Sparse Core Ops, SparseCore 0:
  9.6 20.1 all-gather.35
  110.5 39.6 all-gather.43
  224.5 39.4 all-gather.45
  265.4 22.0 all-gather.37
  288.9 22.5 all-gather.39
  364.8 41.4 all-gather.47
  484.6 39.4 all-gather.49
  526.2 89.5 all-gather.41
  635.2 39.6 all-gather.51
  808.9 38.8 all-gather.55
  849.3 37.0 all-gather.53
  952.1 39.4 all-gather.57
  1059.6 39.4 all-gather.59
  1215.7 39.3 all-gather.61
  1313.0 39.3 all-gather.63
  1355.2 18.0 reduce-scatter.54
  1456.4 19.2 reduce-scatter.52
  1479.6 54.3 reduce-scatter.48
  1538.0 54.7 reduce-scatter.50
  1595.7 22.6 reduce-scatter.42
  1621.1 31.3 reduce-scatter.46
  1655.0 31.4 reduce-scatter.44
  1689.2 28.1 reduce-scatter.40
where the time goes:
time: 1740 us; the launch traced here: 1730 us
  waiting for transfers between devices  587 us (34%)
  blocking collectives  496 us (29%)
  matrix products  259 us (15%)
  local copies, waits for them, and re-layouts  251 us (14%)
  other arithmetic  76.1 us (4%)
  starting transfers between devices  38.9 us (2%)
    unnamed x10, blocking collectives  408 us
    all_gather x6, waiting for transfers between devices, spread_grads(): return lax.all_gather(local_rows, 'tensor', axis=0, tiled=True)  156 us
    all_gather x6, waiting for transfers between devices, spread_rows(): return lax.all_gather(local_rows, 'tensor', axis=0, tiled=True)  155 us
    unnamed x249, local copies, waits for them, and re-layouts  106 us
    unnamed x39, waiting for transfers between devices  96 us
    dot_general x12, matrix products, partial_term(): lax.dot_general(left_rows, right_side, LAST_CONTRACT, preferred_element_t...  41.5 us
    dot_general x3, matrix products, forward_layer(): jnp.dot(normed_two_full, up_weight, preferred_element_type=jnp.float32)  36.1 us
    all_gather x1, blocking collectives, on_device(): lax.all_gather(row_shifts[0], ('dp', 'tensor'), axis=1, tiled=True)  36.1 us
  transfers between devices with their start and end apart: 39, of which 32 were waited for; matrix products, arithmetic and copies ran while one was open for 27% of the time, Pallas kernels for 0%

commit v1 on v0

v1 whole, which is shorter than its diff:
```python
import math

import jax
import jax.numpy as jnp
from jax import lax
from jax.experimental import pallas as pl
from jax.experimental.pallas import tpu as pltpu
from jax.sharding import PartitionSpec as P

D = 1024
HD = 64
SEQ = 197
RP = 208
RC = 16
TILE = 256
SCALE = 0.125
EPS = 1e-06
MESH = pl.DeviceIdType.MESH
BF = jnp.bfloat16
F32 = jnp.float32
NN = (((1,), (0,)), ((), ()))
NT = (((1,), (1,)), ((), ()))
TN = (((0,), (0,)), ((), ()))
VMEM_LIMIT = 60 * 2**20


def mm(a, b, dims):
    return lax.dot_general(a, b, dims, preferred_element_type=F32)


def blk(i, size):
    if isinstance(i, int):
        return pl.ds(i * size, size)
    return pl.ds(pl.multiple_of(i * size, size), size)


class Place:
    def __init__(self, dpn, nz):
        self.Y, self.nz = dpn // 2, nz
        self.x = lax.axis_index("section")
        dp = lax.axis_index("dp")
        self.z = lax.axis_index("tensor")
        self.y, self.c = dp // 2, lax.rem(dp, 2)
        self.j = 2 * self.x + self.c

    def dev(self, x=None, y=None, c=None, z=None):
        x = self.x if x is None else x
        y = self.y if y is None else y
        c = self.c if c is None else c
        z = self.z if z is None else z
        return (x, 2 * y + c, z)

    def cell(self, k):
        jp = lax.rem(self.j + k, 4)
        return jp, jp // 2, lax.rem(jp, 2)

    def yk(self, k):
        return lax.rem(self.y + k, self.Y)

    def zk(self, k):
        return lax.rem(self.z + k, self.nz)

    def barrier(self):
        bar = pltpu.get_barrier_semaphore()
        n = 0
        for k in range(1, 4):
            _, xp, cp = self.cell(k)
            pl.semaphore_signal(bar, inc=1, device_id=self.dev(x=xp, c=cp), device_id_type=MESH)
            n += 1
        for k in range(1, self.nz):
            pl.semaphore_signal(bar, inc=1, device_id=self.dev(z=self.zk(k)), device_id_type=MESH)
            n += 1
        for k in range(1, self.Y):
            pl.semaphore_signal(bar, inc=1, device_id=self.dev(y=self.yk(k)), device_id_type=MESH)
            n += 1
        pl.semaphore_wait(bar, n)


def rcopy(src, dst, ss, rs, dev):
    return pltpu.make_async_remote_copy(
        src_ref=src, dst_ref=dst, send_sem=ss, recv_sem=rs, device_id=dev, device_id_type=MESH
    )


class Exchange:
    def __init__(self, p, op, rb, cs, xr, gs, gr, ss, sr):
        self.p, self.op, self.rb, self.cs, self.xr = p, op, rb, cs, xr
        self.gs, self.gr, self.ss, self.sr = gs, gr, ss, sr

    def rows(self, m, c):
        return blk(2 * m + c, RP)

    def gather(self, buf, s):
        return Gather(self, buf, s)

    def send_core(self, m, s):
        p = self.p
        cp = self._core(m, s)
        cp.start()

    def _core(self, m, s):
        p = self.p
        return rcopy(
            self.op.at[self.rows(m, 1 - p.c)], self.rb.at[m], self.ss.at[s, m], self.sr.at[s, m], p.dev(c=1 - p.c)
        )

    def send_chip(self, s):
        p = self.p
        far = 1 - p.x
        self._core(far, s).wait_recv()
        both = self.op[self.rows(far, p.c), :].astype(F32) + self.rb[far].astype(F32)
        self.cs[...] = both.astype(BF)
        self._chip(s).start()

    def _chip(self, s):
        p = self.p
        return rcopy(self.cs, self.xr, self.ss.at[s, 2], self.sr.at[s, 2], p.dev(x=1 - p.x))

    def wait_sums(self, s):
        self._core(self.p.x, s).wait_recv()
        self._chip(s).wait_recv()

    def sums(self, r):
        p = self.p
        own = self.op[pl.ds(pl.multiple_of((2 * p.x + p.c) * RP + r * RC, RC), RC), :].astype(F32)
        rs = blk(r, RC)
        return own + self.rb[p.x, rs, :].astype(F32) + self.xr[rs, :].astype(F32)

    def done(self, s):
        for m in range(2):
            self._core(m, s).wait_send()
        self._chip(s).wait_send()


class Gather:
    def __init__(self, ex, buf, s):
        p = ex.p
        own, rel = buf.at[ex.rows(p.x, p.c)], buf.at[ex.rows(1 - p.x, p.c)]
        sib = p.dev(c=1 - p.c)
        self.core = rcopy(own, own, ex.gs.at[s, 0], ex.gr.at[s, 0], sib)
        self.chip = rcopy(own, own, ex.gs.at[s, 1], ex.gr.at[s, 1], p.dev(x=1 - p.x))
        self.relay = rcopy(rel, rel, ex.gs.at[s, 2], ex.gr.at[s, 2], sib)

    def start(self):
        self.chip.start()
        self.core.start()

    def near(self):
        self.core.wait_recv()

    def pass_on(self):
        self.chip.wait_recv()
        self.relay.start()

    def far(self):
        self.relay.wait_recv()

    def done(self):
        self.core.wait_send()
        self.chip.wait_send()
        self.relay.wait_send()


def norm_row(v, g, b):
    cen = v - jnp.sum(v, axis=-1, keepdims=True) * (1.0 / D)
    var = jnp.sum(cen * cen, axis=-1, keepdims=True) * (1.0 / D)
    return cen * lax.rsqrt(var + EPS) * g + b


def half(h):
    return blk(h, 2 * RP)


def forward_kernel(dpn, nz, rows):
    Y, R = dpn // 2, rows
    R2 = 2 * R

    def body(
        img, wa, wu, wd, sp,
        lo, o_w, o_nf, o_pr, o_mx, o_n2, o_h, o_gd, o_pb, o_x, o_mid, o_sp,
        W, SPB, SPS, G, NF, PR, MX, N2, H, GD, PB, XO, MID, OUT, LOB, OP, RB, CS, XR,
        red_s, red_r, z_s, z_r, y_s, y_r, ps, pr, gs, gr, ss, sr, lo_s, lo_r, keep,
    ):
        p = Place(dpn, nz)
        x, y, c, z, j = p.x, p.y, p.c, p.z, p.j
        src = (wa, wu, wd)
        ex = Exchange(p, OP, RB, CS, XR, gs, gr, ss, sr)

        XO[0] = jnp.zeros((2, RP, D), BF)
        for m in range(2):
            XO[0, m, 0:SEQ, :] = img[m]
        p.barrier()

        def small_red(k):
            jp, xp, cp = p.cell(k)
            dst = SPB.at[x, y, z, c]
            if k == 0:
                return pltpu.make_async_copy(sp.at[jp], dst, pr.at[x, c])
            return rcopy(sp.at[jp], dst, ps.at[k], pr.at[x, c], p.dev(x=xp, c=cp))

        def small_z(l, k):
            t = SPB.at[l, y, z]
            return rcopy(t, t, ps.at[4 + l * nz + k], pr.at[2 + l, k], p.dev(z=p.zk(k)))

        def small_y(l, k):
            t = SPB.at[l, y]
            return rcopy(t, t, ps.at[4 + 2 * nz + l * Y + k], pr.at[4 + l, k], p.dev(y=p.yk(k)))

        for k in range(4):
            small_red(k).start()

        def red(m, k):
            jp, xp, cp = p.cell(k)
            s = src[m].at[jp] if m == 0 else src[m].at[:, blk(jp, TILE)]
            dst = W.at[x * 3 + m, blk(2 * y + c, R), blk(z, TILE)]
            if k == 0:
                return pltpu.make_async_copy(s, dst, red_r.at[x * 3 + m, c])
            return rcopy(s, dst, red_s.at[m, k], red_r.at[x * 3 + m, c], p.dev(x=xp, c=cp))

        for m in range(3):
            for k in (1, 2, 3, 0):
                red(m, k).start()

        def chunk(lm, zz):
            return W.at[lm, blk(y, R2), blk(zz, TILE)]

        def wz(lm, k):
            t = chunk(lm, z)
            return rcopy(t, t, z_s.at[lm, k], z_r.at[lm, k], p.dev(z=p.zk(k)))

        def wy(lm, kz, ky):
            t = chunk(lm, p.zk(nz - kz))
            return rcopy(t, t, y_s.at[lm, kz, ky], y_r.at[lm, kz, ky], p.dev(y=p.yk(ky)))

        def release(lm):
            for cs_ in range(2):
                t = W.at[lm, blk(2 * y + cs_, R), blk(z, TILE)]
                pltpu.make_async_copy(t, t, red_r.at[lm, cs_]).wait()
            for k in (2, 1, 3):
                if k < nz:
                    wz(lm, k).start()
            for ky in range(1, Y):
                wy(lm, 0, ky).start()

        def hand_on(lm, k):
            wz(lm, k).wait_recv()
            for ky in range(1, Y):
                wy(lm, k, ky).start()

        def hand_all(lm):
            for k in (1, 3, 2):
                hand_on(lm, k)

        def ready(lm):
            for kz in range(nz):
                for ky in range(1, Y):
                    wy(lm, kz, ky).wait_recv()

        for l in range(2):
            for cs_ in range(2):
                t = SPB.at[l, y, z, cs_]
                pltpu.make_async_copy(t, t, pr.at[l, cs_]).wait()
            for k in range(1, nz):
                small_z(l, k).start()
        release(0)
        for l in range(2):
            for k in range(1, nz):
                small_z(l, k).wait_recv()
            for k in range(1, Y):
                small_y(l, k).start()
        for l in range(2):
            for k in range(1, Y):
                small_y(l, k).wait_recv()
            SPS[l] = jnp.sum(SPB[l].astype(F32).reshape(Y * nz * 2, 32, TILE), axis=0)
            for r in range(6):
                for q in range(4):
                    G[l, r : r + 1, q * TILE : (q + 1) * TILE] = SPS[l, 4 * r + q : 4 * r + q + 1, :]

        def put(src_ref, dst_ref, i):
            return pltpu.make_async_copy(src_ref, dst_ref, keep.at[i])

        def ln_first(l, slot, load):
            g, b = G[l, 0:1, :], G[l, 2:3, :]

            def step(r, _):
                v = load(r)
                NF[l, pl.ds(pl.multiple_of(slot * RP + r * RC, RC), RC), :] = norm_row(v, g, b).astype(BF)
                return 0

            lax.fori_loop(0, RP // RC, step, 0)

        def qkv(l, h):
            rows_ = half(h)

            def step(n, _):
                cols = blk(n, TILE)
                t = mm(NF[l, rows_, :], W[3 * l, :, cols], NN)
                PR[l, rows_, cols] = (t + SPS[l, pl.ds(24 + n, 1), :]).astype(BF)
                return 0

            lax.fori_loop(0, 4, step, 0)

        def attend(l, h):
            live = lax.broadcasted_iota(jnp.int32, (RP, RP), 1) < SEQ

            def step(i, _):
                im = 2 * h + i
                rows_ = blk(im, RP)
                for zz in range(4):
                    cols = blk(zz, TILE)
                    t = PR[l, rows_, cols]
                    q, k, v = t[:, 0:HD], t[:, HD : 2 * HD], t[:, 2 * HD : 3 * HD]
                    s = jnp.where(live, mm(q, k, NT) * SCALE, -1e30)
                    w = jnp.exp(s - jnp.max(s, axis=-1, keepdims=True))
                    pb = (w * (1.0 / jnp.sum(w, axis=-1, keepdims=True))).astype(BF)
                    PB[l, 4 * im + zz] = pb
                    o = mm(pb, v, NN).astype(BF)
                    MX[l, rows_, cols] = jnp.concatenate([jnp.zeros((RP, 3 * HD), BF), o], axis=1)
                return 0

            lax.fori_loop(0, 2, step, 0)

        def project(lhs, l, m, h):
            rows_ = half(h)

            def step(n, _):
                cols = blk(n, TILE)
                OP[rows_, cols] = mm(lhs[l, rows_, :], W[3 * l + m, cols, :], NT).astype(BF)
                return 0

            lax.fori_loop(0, 4, step, 0)

        def up(l, h):
            rows_ = half(h)

            def step(n, _):
                cols = blk(n, TILE)
                u = mm(N2[l, rows_, :], W[3 * l + 1, :, cols], NN) + SPS[l, pl.ds(28 + n, 1), :]
                cdf = 0.5 + 0.5 * lax.erf(u * (1.0 / math.sqrt(2.0)))
                H[l, rows_, cols] = (u * cdf).astype(BF)
                GD[l, rows_, cols] = (cdf + u * jnp.exp(-0.5 * u * u) * (1.0 / math.sqrt(2.0 * math.pi))).astype(BF)
                return 0

            lax.fori_loop(0, 4, step, 0)

        near, far = x, 1 - x
        for l in range(2):
            A, U, DN = 3 * l, 3 * l + 1, 3 * l + 2
            if l == 0:
                for m in range(2):
                    ln_first(0, 2 * m + c, lambda r, m=m: XO[0, m, blk(r, RC), :].astype(F32))
                own = [
                    rcopy(NF.at[0, ex.rows(m, c)], NF.at[0, ex.rows(m, c)], gs.at[0, m], gr.at[0, m], p.dev(c=1 - c))
                    for m in range(2)
                ]
                for cp in own:
                    cp.start()
                release(1)
                hand_all(0)
                for cp in own:
                    cp.wait_recv()
            else:
                ln_first(1, 2 * x + c, lambda r: OUT[0, blk(r, RC), :].astype(F32))
                ga = ex.gather(NF.at[1], 2)
                ga.start()
                ga.near()
            ready(A)
            qkv(l, near)
            if l == 1:
                ga.pass_on()
            attend(l, near)
            if l == 0:
                release(2)
                hand_all(1)
            else:
                release(5)
                ga.far()
            qkv(l, far)
            attend(l, far)
            s = 2 * l
            project(MX, l, 0, far)
            ex.send_core(far, s)
            project(MX, l, 0, near)
            ex.send_core(near, s)
            ex.send_chip(s)
            if l == 0:
                release(3)
                hand_all(2)
            else:
                hand_all(4)
            ex.wait_sums(s)
            slot = 2 * x + c
            g, b, sh = G[l, 1:2, :], G[l, 4:5, :], G[l, 3:4, :]

            def second(r, _):
                rs = blk(r, RC)
                v = XO[0, x, rs, :] if l == 0 else OUT[0, rs, :]
                mid = v.astype(F32) + ex.sums(r) + sh
                MID[l, rs, :] = mid
                N2[l, pl.ds(pl.multiple_of(slot * RP + r * RC, RC), RC), :] = norm_row(mid, g, b).astype(BF)
                return 0

            lax.fori_loop(0, RP // RC, second, 0)
            ex.done(s)
            gb = ex.gather(N2.at[l], 1 + 2 * l)
            gb.start()
            ready(U)
            gb.near()
            up(l, near)
            gb.pass_on()
            if l == 0:
                release(4)
                hand_all(3)
            else:
                hand_all(5)
            gb.far()
            up(l, far)
            ready(DN)
            s = 2 * l + 1
            project(H, l, 2, far)
            ex.send_core(far, s)
            project(H, l, 2, near)
            ex.send_core(near, s)
            ex.send_chip(s)
            ex.wait_sums(s)
            sh3 = G[l, 5:6, :]

            def last(r, _):
                rs = blk(r, RC)
                OUT[l, rs, :] = (MID[l, rs, :] + ex.sums(r) + sh3).astype(BF)
                return 0

            lax.fori_loop(0, RP // RC, last, 0)
            ex.done(s)
            if l == 0:
                for cp in own:
                    cp.wait_send()
            else:
                ga.done()
            gb.done()

            @pl.when(x != l)
            def _():
                rcopy(OUT.at[l], LOB, lo_s, lo_r, p.dev(x=1 - x)).start()

            for i, (a, o) in enumerate(
                ((NF, o_nf), (PR, o_pr), (MX, o_mx), (N2, o_n2), (H, o_h), (GD, o_gd), (PB, o_pb), (MID, o_mid))
            ):
                put(a.at[l], o.at[l], 8 * l + i).start()

        put(W, o_w, 16).start()
        put(XO.at[0, x], o_x.at[0], 17).start()
        put(OUT.at[0], o_x.at[1], 18).start()
        put(SPS, o_sp, 19).start()
        for k in range(4):
            if k:
                small_red(k).wait_send()
        for l in range(2):
            for k in range(1, nz):
                small_z(l, k).wait_send()
            for k in range(1, Y):
                small_y(l, k).wait_send()
        for m in range(3):
            for k in range(1, 4):
                red(m, k).wait_send()
        for lm in range(6):
            for k in range(1, nz):
                wz(lm, k).wait_send()
            for kz in range(nz):
                for ky in range(1, Y):
                    wy(lm, kz, ky).wait_send()
        cp = rcopy(OUT.at[x], LOB, lo_s, lo_r, p.dev(x=1 - x))
        cp.wait_recv()
        cp.wait_send()
        lo[x] = OUT[x, 0:SEQ, :]
        lo[1 - x] = LOB[0:SEQ, :]
        for l in range(2):
            for i, (a, o) in enumerate(
                ((NF, o_nf), (PR, o_pr), (MX, o_mx), (N2, o_n2), (H, o_h), (GD, o_gd), (PB, o_pb), (MID, o_mid))
            ):
                put(a.at[l], o.at[l], 8 * l + i).wait()
        put(W, o_w, 16).wait()
        put(XO.at[0, x], o_x.at[0], 17).wait()
        put(OUT.at[0], o_x.at[1], 18).wait()
        put(SPS, o_sp, 19).wait()

    full = (2, 4 * RP, D)
    states = [
        ((6, D, D), BF), (full, BF), (full, BF), (full, BF), (full, BF), (full, BF), (full, BF),
        ((2, 16, RP, RP), BF), ((2, RP, D), BF), ((2, RP, D), F32), ((2, 32, TILE), F32),
    ]
    vm = pl.BlockSpec(memory_space=pltpu.VMEM)
    hbm = pl.BlockSpec(memory_space=pl.ANY)
    dma = pltpu.SemaphoreType.DMA
    return pl.pallas_call(
        body,
        out_shape=[jax.ShapeDtypeStruct((2, SEQ, D), BF)] + [jax.ShapeDtypeStruct(s, t) for s, t in states],
        in_specs=[vm, hbm, hbm, hbm, hbm],
        out_specs=[vm] + [hbm] * len(states),
        scratch_shapes=[
            pltpu.VMEM((6, D, D), BF),
            pltpu.VMEM((2, Y, nz, 2, 32, TILE), BF),
            pltpu.VMEM((2, 32, TILE), F32),
            pltpu.VMEM((2, 8, D), F32),
            pltpu.VMEM(full, BF), pltpu.VMEM(full, BF), pltpu.VMEM(full, BF),
            pltpu.VMEM(full, BF), pltpu.VMEM(full, BF), pltpu.VMEM(full, BF),
            pltpu.VMEM((2, 16, RP, RP), BF),
            pltpu.VMEM((1, 2, RP, D), BF),
            pltpu.VMEM((2, RP, D), F32),
            pltpu.VMEM((2, RP, D), BF),
            pltpu.VMEM((RP, D), BF),
            pltpu.VMEM((4 * RP, D), BF),
            pltpu.VMEM((2, RP, D), BF),
            pltpu.VMEM((RP, D), BF),
            pltpu.VMEM((RP, D), BF),
            dma((3, 4)), dma((6, 2)), dma((6, nz)), dma((6, nz)), dma((6, nz, Y)), dma((6, nz, Y)),
            dma((4 + 2 * nz + 2 * Y,)), dma((6, max(nz, Y, 2))),
            dma((4, 3)), dma((4, 3)), dma((4, 3)), dma((4, 3)), dma, dma, dma((20,)),
        ],
        compiler_params=pltpu.CompilerParams(
            collective_id=0, has_side_effects=True, vmem_limit_bytes=VMEM_LIMIT
        ),
    )


def backward_kernel(dpn, nz, rows):
    Y, R = dpn // 2, rows
    R2 = 2 * R

    def body(
        cot, i_w, i_nf, i_pr, i_mx, i_n2, i_h, i_gd, i_pb, i_x, i_mid, i_sp,
        ig, ga, gu, gd, gs_out,
        W, NF, PR, MX, N2, H, GD, PB, XO, MID, SPS, G,
        GT, GP, GB, GJ, GM, GMID, IGB, LGB, OP, RB, CS, XR,
        DW, YR, ZR, RD, CR, SG, SYR, SZR, SRD, SCR,
        load, gs, gr, ss, sr, lo_s, lo_r,
        y_s, y_r, z_s, z_r, c_s, c_r, sy_s, sy_r, sz_s, sz_r, sc_s, sc_r,
    ):
        p = Place(dpn, nz)
        x, y, c, z, j = p.x, p.y, p.c, p.z, p.j
        ex = Exchange(p, OP, RB, CS, XR, gs, gr, ss, sr)
        near, far = x, 1 - x

        places = {
            "D": (lambda l: i_w.at[3 * l + 2], W.at[2]),
            "GD": (lambda l: i_gd.at[l], GD),
            "H": (lambda l: i_h.at[l], H),
            "U": (lambda l: i_w.at[3 * l + 1], W.at[1]),
            "N2": (lambda l: i_n2.at[l], N2),
            "MID": (lambda l: i_mid.at[l], MID),
            "A": (lambda l: i_w.at[3 * l], W.at[0]),
            "PB": (lambda l: i_pb.at[l], PB),
            "PR": (lambda l: i_pr.at[l], PR),
            "MX": (lambda l: i_mx.at[l], MX),
            "NF": (lambda l: i_nf.at[l], NF),
            "X": (lambda l: i_x.at[l], XO),
        }
        names = list(places)

        def fetch(l, name):
            s, d = places[name]
            return pltpu.make_async_copy(s(l), d, load.at[l, names.index(name)])

        fetch_sp = pltpu.make_async_copy(i_sp, SPS, load.at[0, len(names)])
        fetch_sp.start()
        for name in ("H", "D", "GD", "U", "N2", "MID", "A", "PB", "PR", "MX", "NF", "X"):
            fetch(1, name).start()

        GT[...] = jnp.zeros((4 * RP, D), BF)
        for m in range(2):
            GT[pl.ds(pl.multiple_of((2 * m + c) * RP, RC), SEQ), :] = cot[m]
        SG[...] = jnp.zeros((2, 32, TILE), F32)
        p.barrier()
        first = [
            rcopy(GT.at[ex.rows(m, c)], GT.at[ex.rows(m, c)], gs.at[0, m], gr.at[0, m], p.dev(c=1 - c)) for m in range(2)
        ]
        for cp in first:
            cp.start()
        fetch_sp.wait()
        for l in range(2):
            for r in range(2):
                for q in range(4):
                    G[l, r : r + 1, q * TILE : (q + 1) * TILE] = SPS[l, 4 * r + q : 4 * r + q + 1, :]

        def y_part(l, m, k, kz):
            cols = blk(p.zk(kz), TILE)
            return rcopy(
                DW.at[m, blk(p.yk(k), R2), cols], YR.at[m, k - 1, :, cols],
                y_s.at[3 * l + m, k, kz], y_r.at[3 * l + m, k, kz], p.dev(y=p.yk(k)),
            )

        def z_part(l, m, k):
            return rcopy(
                DW.at[m, blk(y, R2), blk(p.zk(k), TILE)], ZR.at[m, k - 1],
                z_s.at[3 * l + m, k], z_r.at[3 * l + m, k], p.dev(z=p.zk(k)),
            )

        order = (2, 1, 3, 0)

        def y_start(l, m):
            for kz in order:
                for k in range(1, Y):
                    y_part(l, m, k, kz).start()

        def y_sum(l, m):
            for kz in order:
                cols = blk(p.zk(kz), TILE)
                for k in range(1, Y):
                    y_part(l, m, k, kz).wait_recv()
                t = DW[m, blk(y, R2), cols].astype(F32)
                for k in range(1, Y):
                    t = t + YR[m, k - 1, :, cols].astype(F32)
                DW[m, blk(y, R2), cols] = t.astype(BF)
                if kz:
                    z_part(l, m, kz).start()

        def c_part(l, m, cp):
            lm = 3 * l + m
            return rcopy(RD.at[lm, cp], CR.at[m, j], c_s.at[lm, cp], c_r.at[m, j], p.dev(x=l, c=cp))

        def z_sum(l, m):
            for k in range(1, nz):
                z_part(l, m, k).wait_recv()
            t = DW[m, blk(y, R2), blk(z, TILE)].astype(F32)
            for k in range(1, nz):
                t = t + ZR[m, k - 1].astype(F32)
            RD[3 * l + m] = t.astype(BF).reshape(2, R, TILE)
            for cp in range(2):
                mine = jnp.logical_and(x == l, c == cp)

                @pl.when(mine)
                def _():
                    pltpu.make_async_copy(RD.at[3 * l + m, cp], CR.at[m, j], c_r.at[m, j]).start()

                @pl.when(jnp.logical_not(mine))
                def _():
                    c_part(l, m, cp).start()

        def reuse(m):
            for kz in range(nz):
                for k in range(1, Y):
                    y_part(1, m, k, kz).wait_send()
                if kz:
                    z_part(1, m, kz).wait_send()

        def s_y(l, k):
            return rcopy(SG.at[l], SYR.at[l, k - 1], sy_s.at[l, k], sy_r.at[l, k], p.dev(y=p.yk(k)))

        def s_z(l, k):
            return rcopy(SRD.at[l], SZR.at[l, k - 1], sz_s.at[l, k], sz_r.at[l, k], p.dev(z=p.zk(k)))

        def s_c(l, cp):
            return rcopy(SRD.at[2 + l], SCR.at[j], sc_s.at[l, cp], sc_r.at[j], p.dev(x=l, c=cp))

        def s_start(l):
            for k in range(1, Y):
                s_y(l, k).start()

        def s_mid(l):
            for k in range(1, Y):
                s_y(l, k).wait_recv()
            SRD[l] = SG[l] + jnp.sum(SYR[l], axis=0)
            for k in range(1, nz):
                s_z(l, k).start()

        def s_end(l):
            for k in range(1, nz):
                s_z(l, k).wait_recv()
            SRD[2 + l] = SRD[l] + jnp.sum(SZR[l], axis=0)
            for cp in range(2):
                mine = jnp.logical_and(x == l, c == cp)

                @pl.when(mine)
                def _():
                    pltpu.make_async_copy(SRD.at[2 + l], SCR.at[j], sc_r.at[j]).start()

                @pl.when(jnp.logical_not(mine))
                def _():
                    s_c(l, cp).start()

        def add_small(l, row, v):
            SG[l, pl.ds(row, 1), :] += v

        def pre(l, h):
            rows_ = half(h)

            def step(n, _):
                cols = blk(n, TILE)
                t = mm(GT[rows_, :], W[2, :, cols], NN) * GD[rows_, cols].astype(F32)
                gp = t.astype(BF)
                GP[rows_, cols] = gp
                add_small(l, 28 + n, jnp.sum(gp.astype(F32), axis=0, keepdims=True))
                return 0

            lax.fori_loop(0, 4, step, 0)

        def project(lhs, m, h):
            rows_ = half(h)

            def step(n, _):
                cols = blk(n, TILE)
                OP[rows_, cols] = mm(lhs[rows_, :], W[m, cols, :], NT).astype(BF)
                return 0

            lax.fori_loop(0, 4, step, 0)

        def weight_grad(m, pairs):
            def step(r, _):
                cols = blk(r, TILE)
                t = mm(pairs[0][0][:, cols], pairs[0][1][...], TN)
                for a, b in pairs[1:]:
                    t = t + mm(a[:, cols], b[...], TN)
                DW[m, cols, :] = t.astype(BF)
                return 0

            lax.fori_loop(0, 4, step, 0)

        def mixed_grad(h):
            rows_ = half(h)

            def step(n, _):
                cols = blk(n, TILE)
                GM[rows_, cols] = mm(GB[rows_, :], W[0, :, cols], NN).astype(BF)
                return 0

            lax.fori_loop(0, 4, step, 0)

        def attend_back(l, h):
            def step(i, _):
                im = 2 * h + i
                rows_ = blk(im, RP)
                for zz in range(4):
                    cols = blk(zz, TILE)
                    t = PR[rows_, cols]
                    q, k, v = t[:, 0:HD], t[:, HD : 2 * HD], t[:, 2 * HD : 3 * HD]
                    gm = GM[rows_, cols][:, 3 * HD : 4 * HD]
                    pb = PB[4 * im + zz]
                    pf = pb.astype(F32)
                    gp = mm(gm, v, NT)
                    cen = jnp.sum(pf * gp, axis=-1, keepdims=True)
                    gsc = (pf * (gp - cen)).astype(BF)
                    gq = mm(gsc, k, NN) * SCALE
                    gk = mm(gsc, q, TN) * SCALE
                    gv = mm(pb, gm, TN)
                    out = jnp.concatenate([gq, gk, gv, jnp.zeros((RP, HD), F32)], axis=1).astype(BF)
                    GJ[rows_, cols] = out
                    add_small(l, 24 + zz, jnp.sum(out.astype(F32), axis=0, keepdims=True))
                return 0

            lax.fori_loop(0, 2, step, 0)

        def fold(v):
            return v[0:8] + v[8:16]

        def put_small(l, row, acc):
            t = jnp.sum(acc, axis=0, keepdims=True)
            for q in range(4):
                add_small(l, 4 * row + q, t[:, q * TILE : (q + 1) * TILE])

        def norm_back(v, g, dy):
            cen = v - jnp.sum(v, axis=-1, keepdims=True) * (1.0 / D)
            rstd = lax.rsqrt(jnp.sum(cen * cen, axis=-1, keepdims=True) * (1.0 / D) + EPS)
            hat = cen * rstd
            dh = dy * g
            a = jnp.sum(dh, axis=-1, keepdims=True) * (1.0 / D)
            b = jnp.sum(dh * hat, axis=-1, keepdims=True) * (1.0 / D)
            return rstd * (dh - a - hat * b), dy * hat

        slot = 2 * x + c

        def own_rows(r):
            return pl.ds(pl.multiple_of(slot * RP + r * RC, RC), RC)

        zero8 = jnp.zeros((8, D), F32)

        for l in (1, 0):
            if l == 1:
                for cp in first:
                    cp.wait_recv()
                fetch(1, "H").wait()
                weight_grad(2, [(GT, H)])
                y_start(1, 2)
                fetch(0, "H").start()
                fetch(1, "D").wait()
                fetch(1, "GD").wait()
                pre(1, far)
                pre(1, near)
                for cp in first:
                    cp.wait_send()
            else:
                gt = ex.gather(GT, 1)
                gt.start()
                z_sum(1, 1)
                y_sum(1, 0)
                fetch(0, "D").wait()
                fetch(0, "GD").wait()
                gt.near()
                pre(0, near)
                gt.pass_on()
                gt.far()
                pre(0, far)
            fetch(l, "U").wait()
            s = 2 * (1 - l)
            project(GP, 1, far)
            ex.send_core(far, s)
            project(GP, 1, near)
            ex.send_core(near, s)
            ex.send_chip(s)
            if l == 1:
                for name in ("D", "GD", "U"):
                    fetch(0, name).start()
                fetch(1, "N2").wait()
                weight_grad(1, [(N2, GP)])
                y_start(1, 1)
                fetch(0, "N2").start()
            else:
                z_sum(1, 0)
                s_end(1)
                reuse(2)
                fetch(0, "H").wait()
                weight_grad(2, [(GT, H)])
                y_start(0, 2)
            ex.wait_sums(s)
            fetch(l, "MID").wait()

            def mid_back(r, acc):
                rs = blk(r, RC)
                dy = ex.sums(r)
                top = GT[own_rows(r), :].astype(F32)
                dx, dg = norm_back(MID[rs, :], G[l, 1:2, :], dy)
                gmid = top + dx
                GMID[rs, :] = gmid
                GB[own_rows(r), :] = gmid.astype(BF)
                return acc[0] + fold(dg), acc[1] + fold(dy), acc[2] + fold(gmid), acc[3] + fold(top)

            acc = lax.fori_loop(0, RP // RC, mid_back, (zero8,) * 4)
            put_small(l, 1, acc[0])
            put_small(l, 4, acc[1])
            put_small(l, 3, acc[2])
            put_small(l, 5, acc[3])
            ex.done(s)
            gb = ex.gather(GB, 2 + (1 - l))
            gb.start()
            if l == 1:
                fetch(0, "MID").start()
                y_sum(1, 2)
            else:
                reuse(1)
                fetch(0, "N2").wait()
                weight_grad(1, [(N2, GP)])
                y_start(0, 1)
            fetch(l, "A").wait()
            fetch(l, "PR").wait()
            fetch(l, "PB").wait()
            gb.near()
            mixed_grad(near)
            gb.pass_on()
            attend_back(l, near)
            if l == 1:
                y_sum(1, 1)
            else:
                y_sum(0, 2)
            gb.far()
            mixed_grad(far)
            attend_back(l, far)
            fetch(l, "MX").wait()
            fetch(l, "NF").wait()
            if l == 0:
                reuse(0)
                weight_grad(0, [(NF, GJ), (GB, MX)])
                y_start(0, 0)
            s = 2 * (1 - l) + 1
            project(GJ, 0, far)
            ex.send_core(far, s)
            project(GJ, 0, near)
            ex.send_core(near, s)
            ex.send_chip(s)
            if l == 1:
                weight_grad(0, [(NF, GJ), (GB, MX)])
                z_sum(1, 2)
                y_start(1, 0)
                for name in ("A", "PB", "PR", "MX", "NF"):
                    fetch(0, name).start()
            else:
                y_sum(0, 1)
                z_sum(0, 2)
            ex.wait_sums(s)
            fetch(l, "X").wait()

            def first_back(r, acc):
                rs = blk(r, RC)
                dy = ex.sums(r)
                dx, dg = norm_back(XO[rs, :].astype(F32), G[l, 0:1, :], dy)
                gx = (GMID[rs, :] + dx).astype(BF)
                IGB[l, rs, :] = gx
                if l == 1:
                    GT[own_rows(r), :] = gx
                return acc[0] + fold(dg), acc[1] + fold(dy)

            acc = lax.fori_loop(0, RP // RC, first_back, (zero8,) * 2)
            put_small(l, 0, acc[0])
            put_small(l, 2, acc[1])
            ex.done(s)
            gb.done()
            if l == 1:
                fetch(0, "X").start()
            else:
                gt.done()
            s_start(l)

            @pl.when(x != l)
            def _():
                rcopy(IGB.at[l], LGB, lo_s, lo_r, p.dev(x=1 - x)).start()

            if l == 1:
                s_mid(1)

        s_mid(0)
        y_sum(0, 0)
        z_sum(0, 1)
        s_end(0)
        z_sum(0, 0)
        cp = rcopy(IGB.at[x], LGB, lo_s, lo_r, p.dev(x=1 - x))
        cp.wait_recv()
        cp.wait_send()
        ig[x] = IGB[x, 0:SEQ, :]
        ig[1 - x] = LGB[0:SEQ, :]
        for m in (2, 1, 0):
            for jj in range(4):
                pltpu.make_async_copy(CR.at[m, jj], CR.at[m, jj], c_r.at[m, jj]).wait()
                t = CR[m, jj].astype(F32)
                if m == 0:
                    ga[jj] = t
                elif m == 1:
                    gu[:, jj * TILE : (jj + 1) * TILE] = t
                else:
                    gd[:, jj * TILE : (jj + 1) * TILE] = t
        for jj in range(4):
            pltpu.make_async_copy(SCR.at[jj], SCR.at[jj], sc_r.at[jj]).wait()
            gs_out[jj] = SCR[jj]
        for m in range(3):
            for kz in range(nz):
                for k in range(1, Y):
                    y_part(0, m, k, kz).wait_send()
                if kz:
                    z_part(0, m, kz).wait_send()
        for l in range(2):
            for k in range(1, Y):
                s_y(l, k).wait_send()
            for k in range(1, nz):
                s_z(l, k).wait_send()
            for cp in range(2):

                @pl.when(jnp.logical_not(jnp.logical_and(x == l, c == cp)))
                def _():
                    s_c(l, cp).wait_send()
                    for m in range(3):
                        c_part(l, m, cp).wait_send()

    full = (4 * RP, D)
    vm = pl.BlockSpec(memory_space=pltpu.VMEM)
    hbm = pl.BlockSpec(memory_space=pl.ANY)
    dma = pltpu.SemaphoreType.DMA
    return pl.pallas_call(
        body,
        out_shape=[
            jax.ShapeDtypeStruct((2, SEQ, D), BF),
            jax.ShapeDtypeStruct((4, R, TILE), F32),
            jax.ShapeDtypeStruct((R, D), F32),
            jax.ShapeDtypeStruct((R, D), F32),
            jax.ShapeDtypeStruct((4, 32, TILE), F32),
        ],
        in_specs=[vm] + [hbm] * 11,
        out_specs=[vm] * 5,
        scratch_shapes=[
            pltpu.VMEM((3, D, D), BF),
            pltpu.VMEM(full, BF), pltpu.VMEM(full, BF), pltpu.VMEM(full, BF),
            pltpu.VMEM(full, BF), pltpu.VMEM(full, BF), pltpu.VMEM(full, BF),
            pltpu.VMEM((16, RP, RP), BF),
            pltpu.VMEM((RP, D), BF),
            pltpu.VMEM((RP, D), F32),
            pltpu.VMEM((2, 32, TILE), F32),
            pltpu.VMEM((2, 8, D), F32),
            pltpu.VMEM(full, BF), pltpu.VMEM(full, BF), pltpu.VMEM(full, BF),
            pltpu.VMEM(full, BF), pltpu.VMEM(full, BF),
            pltpu.VMEM((RP, D), F32),
            pltpu.VMEM((2, RP, D), BF),
            pltpu.VMEM((RP, D), BF),
            pltpu.VMEM(full, BF),
            pltpu.VMEM((2, RP, D), BF),
            pltpu.VMEM((RP, D), BF),
            pltpu.VMEM((RP, D), BF),
            pltpu.VMEM((3, D, D), BF),
            pltpu.VMEM((3, Y - 1, R2, D), BF),
            pltpu.VMEM((3, nz - 1, R2, TILE), BF),
            pltpu.VMEM((6, 2, R, TILE), BF),
            pltpu.VMEM((3, 4, R, TILE), BF),
            pltpu.VMEM((2, 32, TILE), F32),
            pltpu.VMEM((2, Y - 1, 32, TILE), F32),
            pltpu.VMEM((2, nz - 1, 32, TILE), F32),
            pltpu.VMEM((4, 32, TILE), F32),
            pltpu.VMEM((4, 32, TILE), F32),
            dma((2, 13)), dma((4, 3)), dma((4, 3)), dma((4, 3)), dma((4, 3)), dma, dma,
            dma((6, Y, nz)), dma((6, Y, nz)), dma((6, nz)), dma((6, nz)), dma((6, 2)), dma((3, 4)),
            dma((2, Y)), dma((2, Y)), dma((2, nz)), dma((2, nz)), dma((2, 2)), dma((4,)),
        ],
        compiler_params=pltpu.CompilerParams(
            collective_id=1, has_side_effects=True, vmem_limit_bytes=VMEM_LIMIT
        ),
    )


def small_pack(norm_gains, row_shifts, head_bias, unit_bias, dpn, nz):
    dp, z = lax.axis_index("dp"), lax.axis_index("tensor")
    rows = jnp.concatenate([norm_gains[0], row_shifts[0]], axis=0)
    w = rows.shape[1]
    rows = lax.dynamic_update_slice(jnp.zeros((6, D), BF), rows, (0, (dp * nz + z) * w)).reshape(1, 24, TILE)
    hw, uw = head_bias.shape[3], unit_bias.shape[2]
    head = jnp.zeros((4, 4, TILE), BF)
    head = lax.dynamic_update_slice(head, head_bias[0, 0][:, None], (0, z, dp * hw))
    head = lax.dynamic_update_slice(head, head_bias[0, 1][:, None], (0, z, 2 * HD + dp * hw))
    unit = lax.dynamic_update_slice(jnp.zeros((4, 4, TILE), BF), unit_bias[0][:, None], (0, z, dp * uw))
    return jnp.concatenate([jnp.broadcast_to(rows, (4, 24, TILE)), head, unit], axis=1)


def solution(mesh):
    dpn, nz = mesh.shape["dp"], mesh.shape["tensor"]

    def on_device(
        images_in, cotangent, w_qkv, w_out, w_up, w_down, norm_gains, row_shifts, head_bias, unit_bias
    ):
        R = w_up.shape[1]
        qkv = w_qkv[0].reshape(R, 3, 4, HD).transpose(2, 0, 1, 3).reshape(4, R, 3 * HD)
        wo = w_out[0].reshape(R, 4, HD).transpose(1, 0, 2)
        wa = jnp.concatenate([qkv, wo], axis=2)
        sp = small_pack(norm_gains, row_shifts, head_bias, unit_bias, dpn, nz)
        res = forward_kernel(dpn, nz, R)(images_in, wa, w_up[0], w_down[0], sp)
        ig, ga, gu, gd, gs = backward_kernel(dpn, nz, R)(cotangent, *res[1:])
        dp, z = lax.axis_index("dp"), lax.axis_index("tensor")
        g_qkv = ga[:, :, : 3 * HD].reshape(4, R, 3, HD).transpose(1, 2, 0, 3).reshape(w_qkv.shape)
        g_out = ga[:, :, 3 * HD :].transpose(1, 0, 2).reshape(w_out.shape)
        w, hw, uw = norm_gains.shape[2], head_bias.shape[3], unit_bias.shape[2]
        rows = lax.dynamic_slice(jnp.sum(gs[:, :24], axis=0).reshape(6, D), (0, (dp * nz + z) * w), (6, w))
        head = lax.dynamic_slice(gs, (0, 24 + z, 0), (4, 1, TILE))[:, 0]
        unit = lax.dynamic_slice(gs, (0, 28 + z, dp * uw), (4, 1, uw))[:, 0]
        g_head = jnp.stack([lax.dynamic_slice(head, (0, o + dp * hw), (4, hw)) for o in (0, 2 * HD)])
        return (
            res[0][None], ig[None], g_qkv, g_out, gu[None], gd[None],
            rows[None, :2], rows[None, 2:], g_head[None], unit[None],
        )

    in_specs = (
        P(None, ("dp", "tensor"), None),
        P(None, ("dp", "tensor"), None),
        P("section", "dp", None, "tensor"),
        P("section", "dp", "tensor"),
        P("section", "dp", "tensor"),
        P("section", "dp", "tensor"),
        P("section", None, ("dp", "tensor")),
        P("section", None, ("dp", "tensor")),
        P("section", None, "tensor", "dp"),
        P("section", "tensor", "dp"),
    )
    out_specs = (
        P("section", None, ("dp", "tensor"), None),
        P("section", None, ("dp", "tensor"), None),
        P("section", "dp", None, "tensor"),
        P("section", "dp", "tensor"),
        P("section", "dp", "tensor"),
        P("section", "dp", "tensor"),
        P("section", None, ("dp", "tensor")),
        P("section", None, ("dp", "tensor")),
        P("section", None, "tensor", "dp"),
        P("section", "tensor", "dp"),
    )
    return jax.shard_map(
        on_device, mesh=mesh, in_specs=in_specs, out_specs=out_specs, check_vma=False
    )
```

time: 1740 us -> 488 us (0.28)
  waiting for transfers between devices: 587 us -> 0 us
  blocking collectives: 496 us -> 0 us
  Pallas kernels: 0 us -> 457 us
  matrix products: 259 us -> 0 us
  local copies, waits for them, and re-layouts: 251 us -> 24.8 us
  other arithmetic: 76.1 us -> 2.22 us
  starting transfers between devices: 38.9 us -> 0 us
    pallas_call x0 -> x2, Pallas kernels: none -> 457 us  [the longest x1 229 us: on_device(): ig, ga, gu, gd, gs = backward_kernel(dpn, nz, R)(cotangent, *res[1:])]
    unnamed x10 -> x0, blocking collectives: 408 us -> none
    all_gather x15 -> x0, waiting for transfers between devices: 343 us -> none  [the longest x6 156 us: spread_grads(): return lax.all_gather(local_rows, 'tensor', axis=0, tiled=True)]
    dot_general x120 -> x0, matrix products: 259 us -> none  [the longest x12 41.5 us: partial_term(): lax.dot_general(left_rows, right_side, LAST_CONTRACT, preferred_element_t...]
    reduce_scatter x4 -> x0, waiting for transfers between devices: 117 us -> none  [the longest x1 32.5 us: reduce_grads(): lax.psum_scatter(weight_grads[3].astype(jnp.bfloat16), 'dp', scatter_dime...]
    unnamed x39 -> x0, waiting for transfers between devices: 96 us -> none
    all_gather x5 -> x0, blocking collectives: 88.1 us -> none  [the longest x1 36.1 us: on_device(): lax.all_gather(row_shifts[0], ('dp', 'tensor'), axis=1, tiled=True)]
    unnamed x249 -> x24, local copies, waits for them, and re-layouts: 106 us -> 18 us
  transfers between devices with their start and end apart: 39 -> 0, of which waited for: 32 -> 0; matrix products, arithmetic and copies ran while one was open for 27% -> 0% of each run, Pallas kernels for 0% -> 0%
where the time goes in v1:
time: 488 us; the launch traced here: 485 us
  Pallas kernels  457 us (94%)
  local copies, waits for them, and re-layouts  24.8 us (5%)
    pallas_call x1, Pallas kernels, on_device(): ig, ga, gu, gd, gs = backward_kernel(dpn, nz, R)(cotangent, *res[1:])  229 us
    pallas_call x1, Pallas kernels, on_device(): res = forward_kernel(dpn, nz, R)(images_in, wa, w_up[0], w_down[0], sp)  228 us
    unnamed x24, local copies, waits for them, and re-layouts  18 us

profile of v1, /device:TPU:21, one launch (start us, length us, event | category | flops | bytes accessed | tf_op | source)
XLA Modules:
  0.0 485.0 jit_solution(4359297956377298722)
XLA Ops:
  0.6 0.0 copy-start.4
  0.7 0.0 copy-start.3
  0.7 0.0 copy-start.5
  0.7 0.0 copy-start.6
  0.7 2.3 copy.36.img
  3.0 1.0 copy.30
  4.0 0.2 copy.31
  4.1 1.2 copy.28
  5.3 0.0 copy-start.1
  5.4 0.2 copy.32
  5.6 1.0 pad_maximum_fusion.wa
  6.5 0.0 copy-done.4
  6.5 0.7 dynamic_update_slice.15
  7.3 0.0 copy-done.3
  7.3 0.8 dynamic_update_slice.13
  8.1 0.7 dynamic_update_slice.14
  8.9 0.0 copy-done.5
  8.9 0.0 copy-done.6
  8.9 0.1 dynamic_update_slice.12
  9.1 0.6 pad_maximum_fusion.1.sp
  9.8 228.4 %shard_map.177 = (bf16[2,197,1024]{2,1,0:T(8,128)(2,1)}, bf16[6,1024,1024]{2,1,0:T(8,128)(2,1)}, bf16[2,832,1024]{2,1,0:T(8,128)(2,1)}, bf16[2,832,1024]{2,1,0:T...) custom-call(bf16[2,197,1024]{2,1,0:T(8,128)(2,1)} %copy.36.img, ...), custom_call_target="tpu_custom_call" | custom-call | tf_op jit(solution)/shard_map/pallas_call | solution.py:1037
  238.2 2.9 copy.41
  241.0 0.0 copy-done.1
  241.0 1.1 copy.37.cot
  242.1 228.7 %shard_map.178 = (bf16[2,197,1024]{2,1,0:T(8,128)(2,1)}, f32[4,256,256]{2,1,0:T(8,128)}, f32[256,1024]{1,0:T(8,128)}, f32[256,1024]{1,0:T(8,128)}, f32[4,32,256]{2,1,0:T(8,128)}) custom-call(bf16[2,197,1024]{2,1,0:T(8,128)(2,1)} %copy.37.cot, bf16[6,1024,1024]{2,1,0:T(8,128)(2,1)} %get-tuple-element.28.i_w, bf16[2,832,1024]{2,1,0:T(8,128)(2,1)} %get-tuple-element.29.i_nf, ...), custom_call_target="tpu_custom_call" | custom-call | tf_op jit(solution)/shard_map/pallas_call | solution.py:1038
  470.9 0.0 copy-start
  470.9 3.0 copy.42
  473.8 0.0 copy-start.2
  473.8 1.6 copy.38
  475.4 0.1 copy.39
  475.5 1.1 copy.43
  476.6 0.0 copy-done
  476.6 0.2 slice_bitcast_fusion
  476.8 0.2 copy.40
  477.0 0.8 copy.44
  477.8 0.0 copy-done.2
  477.9 0.1 constant_dynamic-slice_fusion.3
  477.9 0.6 slice_bitcast_fusion.2
  478.5 0.6 slice_bitcast_fusion.1
  479.1 0.1 constant_dynamic-slice_fusion.2
  479.2 0.6 maximum_bitcast_fusion
  479.8 0.7 constant_dynamic-slice_fusion
  480.4 2.3 copy.51
  482.7 2.3 copy.52
  (13 shorter events, 0.1 us)
Async XLA Ops:
  0.6 5.9 %copy-start.4 = (bf16[1,4,64]{2,1,0:T(4,128)(2,1)S(1)}, bf16[1,4,64]{2,1,0:T(4,128)(2,1)}, u32[]{:S(2)}) copy-start(bf16[1,4,64]{2,1,0:T(4,128)(2,1)} %param.19) | copy-start | bytes 1540
  0.7 6.6 %copy-start.3 = (bf16[1,2,4,16]{3,2,1,0:T(4,128)(2,1)S(1)}, bf16[1,2,4,16]{3,2,1,0:T(4,128)(2,1)}, u32[]{:S(2)}) copy-start(bf16[1,2,4,16]{3,2,1,0:T(4,128)(2,1)} %param.18) | copy-start | bytes 772
  0.7 8.2 %copy-start.5 = (bf16[1,4,64]{2,1,0:T(4,128)(2,1)S(1)}, bf16[1,4,64]{2,1,0:T(4,128)(2,1)}, u32[]{:S(2)}) copy-start(bf16[1,4,64]{2,1,0:T(4,128)(2,1)} %param.17) | copy-start | bytes 1540
  0.7 8.2 %copy-start.6 = (bf16[1,2,64]{2,1,0:T(2,128)(2,1)S(1)}, bf16[1,2,64]{2,1,0:T(2,128)(2,1)}, u32[]{:S(2)}) copy-start(bf16[1,2,64]{2,1,0:T(2,128)(2,1)} %param.16) | copy-start | bytes 772
  5.3 235.7 %copy-start.1 = (bf16[2,197,1024]{2,0,1:T(2,128)(2,1)S(1)}, bf16[2,197,1024]{2,0,1:T(2,128)(2,1)}, u32[]{:S(2)}) copy-start(bf16[2,197,1024]{2,0,1:T(2,128)(2,1)} %param.11) | copy-start | bytes 2420740
  470.9 5.8 %copy-start = (f32[4,256,256]{2,1,0:T(8,128)S(1)}, f32[4,256,256]{2,1,0:T(8,128)}, u32[]{:S(2)}) copy-start(f32[4,256,256]{2,1,0:T(8,128)} %get-tuple-element.40) | copy-start | bytes 3145732
  473.8 4.0 copy-start.2

commit v2 on v0

v2 whole, which is shorter than its diff:
```python
import math
import types

import jax
import jax.numpy as jnp
from jax import lax
from jax.experimental import pallas as pl
from jax.experimental.pallas import tpu as pltpu
from jax.sharding import PartitionSpec as P

D = 1024
HD = 64
SEQ = 197
RP = 208
RC = 16
TILE = 256
SCALE = 0.125
EPS = 1e-06
MESH = pl.DeviceIdType.MESH
BF = jnp.bfloat16
F32 = jnp.float32
NN = (((1,), (0,)), ((), ()))
NT = (((1,), (1,)), ((), ()))
TN = (((0,), (0,)), ((), ()))
VMEM_LIMIT = 62 * 2**20


def mm(a, b, dims):
    return lax.dot_general(a, b, dims, preferred_element_type=F32)


def blk(i, size):
    if isinstance(i, int):
        return pl.ds(i * size, size)
    return pl.ds(pl.multiple_of(i * size, size), size)


class Place:
    def __init__(self, dpn, nz):
        self.Y, self.nz = dpn // 2, nz
        self.x = lax.axis_index("section")
        dp = lax.axis_index("dp")
        self.z = lax.axis_index("tensor")
        self.y, self.c = dp // 2, lax.rem(dp, 2)
        self.j = 2 * self.x + self.c

    def dev(self, x=None, y=None, c=None, z=None):
        x = self.x if x is None else x
        y = self.y if y is None else y
        c = self.c if c is None else c
        z = self.z if z is None else z
        return (x, 2 * y + c, z)

    def cell(self, k):
        jp = lax.rem(self.j + k, 4)
        return jp, jp // 2, lax.rem(jp, 2)

    def yk(self, k):
        return lax.rem(self.y + k, self.Y)

    def zk(self, k):
        return lax.rem(self.z + k, self.nz)

    def barrier(self):
        bar = pltpu.get_barrier_semaphore()
        n = 0
        for k in range(1, 4):
            _, xp, cp = self.cell(k)
            pl.semaphore_signal(bar, inc=1, device_id=self.dev(x=xp, c=cp), device_id_type=MESH)
            n += 1
        for k in range(1, self.nz):
            pl.semaphore_signal(bar, inc=1, device_id=self.dev(z=self.zk(k)), device_id_type=MESH)
            n += 1
        for k in range(1, self.Y):
            pl.semaphore_signal(bar, inc=1, device_id=self.dev(y=self.yk(k)), device_id_type=MESH)
            n += 1
        pl.semaphore_wait(bar, n)


def rcopy(src, dst, ss, rs, dev):
    return pltpu.make_async_remote_copy(
        src_ref=src, dst_ref=dst, send_sem=ss, recv_sem=rs, device_id=dev, device_id_type=MESH
    )


def norm_row(v, g, b):
    cen = v - jnp.sum(v, axis=-1, keepdims=True) * (1.0 / D)
    var = jnp.sum(cen * cen, axis=-1, keepdims=True) * (1.0 / D)
    return cen * lax.rsqrt(var + EPS) * g + b


def norm_back(v, g, dy):
    cen = v - jnp.sum(v, axis=-1, keepdims=True) * (1.0 / D)
    rstd = lax.rsqrt(jnp.sum(cen * cen, axis=-1, keepdims=True) * (1.0 / D) + EPS)
    hat = cen * rstd
    dh = dy * g
    a = jnp.sum(dh, axis=-1, keepdims=True) * (1.0 / D)
    b = jnp.sum(dh * hat, axis=-1, keepdims=True) * (1.0 / D)
    return rstd * (dh - a - hat * b), dy * hat


def fold(v):
    return v[0:8] + v[8:16]


def half(g):
    return blk(g, 2 * RP)


def row(g, m):
    return blk(2 * g + m, RP)


def both_layers(dpn, nz, rows):
    Y, R = dpn // 2, rows
    R2 = 2 * R
    full = (4 * RP, D)
    dma = pltpu.SemaphoreType.DMA
    inputs = ["img", "cot", "wa", "wu", "wd", "sp"]
    outputs = {
        "lo": ((2, SEQ, D), BF), "ig": ((2, SEQ, D), BF), "ga": ((4, R, TILE), F32), "gu": ((R, D), F32),
        "gd": ((R, D), F32), "gs_out": ((4, 32, TILE), F32),
    }
    spilled = {"NF": full, "PR": full, "N2": full, "H": full, "GD": full, "PB": (16, RP, RP)}
    vmem = {
        "W": ((6, D, D), BF), "DX": ((D, D), BF), "SPB": ((2, Y, nz, 2, 32, TILE), BF), "SPS": ((2, 32, TILE), F32),
        "G": ((2, 8, D), F32), "NF": (full, BF), "PR": (full, BF), "N2": (full, BF), "H": (full, BF), "GD": (full, BF),
        "PB": ((16, RP, RP), BF), "MX": (full, BF), "GT": (full, BF), "OP": (full, BF), "RB": ((2, 2, RP, D), BF),
        "CS": ((2, RP, D), BF), "XR": ((2, RP, D), BF), "XO": ((2, RP, D), BF), "MID": ((2, RP, D), F32),
        "OUT": ((2, RP, D), BF), "LOB": ((RP, D), BF), "GMID": ((RP, D), F32), "IGB": ((2, RP, D), BF),
        "LGB": ((RP, D), BF), "YR": ((3, Y - 1, R2, D), BF), "ZR": ((6, nz - 1, R2, TILE), BF),
        "RD": ((6, 2, R, TILE), BF), "CR": ((3, 4, R, TILE), BF), "SG": ((2, 32, TILE), F32),
        "SYR": ((2, Y - 1, 32, TILE), F32), "SZR": ((2, nz - 1, 32, TILE), F32), "SRD": ((4, 32, TILE), F32),
        "SCR": ((4, 32, TILE), F32),
    }
    sems = {
        "red_s": (3, 4), "red_r": (6, 2), "fz_s": (6, 4), "fz_r": (6, 4), "fy_s": (6, 4, Y), "fy_r": (6, 4, Y),
        "ps": (4 + 2 * nz + 2 * Y,), "pr": (6, max(nz, Y, 2)), "gs": (8, 3), "gr": (8, 3), "ss": (8, 3), "sr": (8, 3),
        "lo_s": (2,), "lo_r": (2,), "keep": (2, 6), "y_s": (6, Y, nz), "y_r": (6, Y, nz), "z_s": (6, nz), "z_r": (6, nz),
        "c_s": (6, 2), "c_r": (3, 4), "sy_s": (2, Y), "sy_r": (2, Y), "sz_s": (2, nz), "sz_r": (2, nz), "sc_s": (2, 2),
        "sc_r": (4,),
    }
    names = inputs + list(outputs) + ["o_" + n for n in spilled] + list(vmem) + list(sems)

    def body(*refs):
        t = types.SimpleNamespace(**dict(zip(names, refs)))
        p = Place(dpn, nz)
        x, y, c, z, j = p.x, p.y, p.c, p.z, p.j
        near, far = x, 1 - x
        W, OP, RB, CS, XR = t.W, t.OP, t.RB, t.CS, t.XR

        def core_part(g, m, s):
            return rcopy(OP.at[row(g, m)], RB.at[int(s == 3), m], t.ss.at[s, m], t.sr.at[s, m], p.dev(c=1 - c))

        def chip_part(s):
            k = int(s == 3)
            return rcopy(CS.at[k], XR.at[k], t.ss.at[s, 2], t.sr.at[s, 2], p.dev(x=1 - x))

        def rs_out(g, s):
            @pl.when(c != g)
            def _():
                core_part(g, far, s).start()
                core_part(g, near, s).start()

            @pl.when(c == g)
            def _():
                core_part(g, far, s).wait_recv()
                k = int(s == 3)
                CS[k] = (OP[row(g, far), :].astype(F32) + RB[k, far].astype(F32)).astype(BF)
                chip_part(s).start()

        def rs_in(g, s, fn):
            @pl.when(c == g)
            def _():
                core_part(g, near, s).wait_recv()
                chip_part(s).wait_recv()
                fn()

        def rs_done(g, s):
            @pl.when(c != g)
            def _():
                for m in range(2):
                    core_part(g, m, s).wait_send()

            @pl.when(c == g)
            def _():
                chip_part(s).wait_send()

        def sums(g, r):
            rs = blk(r, RC)
            own = OP[pl.ds(pl.multiple_of((2 * g + x) * RP + r * RC, RC), RC), :].astype(F32)
            return own + RB[0, x, rs, :].astype(F32) + XR[0, rs, :].astype(F32)

        def ag_part(buf, g, s, k):
            b = buf.at[row(g, far if k == 2 else near)]
            return rcopy(b, b, t.gs.at[s, k], t.gr.at[s, k], p.dev(x=1 - x) if k == 1 else p.dev(c=1 - c))

        def ag_send(buf, g, s):
            ag_part(buf, g, s, 1).start()
            ag_part(buf, g, s, 0).start()

        def ag_mid(buf, g, s):
            @pl.when(c == g)
            def _():
                ag_part(buf, g, s, 1).wait_recv()
                ag_part(buf, g, s, 2).start()

        def ag_in(buf, g, s):
            @pl.when(c != g)
            def _():
                ag_part(buf, g, s, 0).wait_recv()
                ag_part(buf, g, s, 2).wait_recv()

        def ag_done(buf, s):
            for g in range(2):

                @pl.when(c == g)
                def _():
                    for k in range(3):
                        ag_part(buf, g, s, k).wait_send()

        def ag_local(buf, s):
            return [
                rcopy(buf.at[row(c, m)], buf.at[row(c, m)], t.gs.at[s, m], t.gr.at[s, m], p.dev(c=1 - c))
                for m in range(2)
            ]

        def small_red(k):
            jp, xp, cp = p.cell(k)
            dst = t.SPB.at[x, y, z, c]
            if k == 0:
                return pltpu.make_async_copy(t.sp.at[jp], dst, t.pr.at[x, c])
            return rcopy(t.sp.at[jp], dst, t.ps.at[k], t.pr.at[x, c], p.dev(x=xp, c=cp))

        def small_z(l, k):
            b = t.SPB.at[l, y, z]
            return rcopy(b, b, t.ps.at[4 + l * nz + k], t.pr.at[2 + l, k], p.dev(z=p.zk(k)))

        def small_y(l, k):
            b = t.SPB.at[l, y]
            return rcopy(b, b, t.ps.at[4 + 2 * nz + l * Y + k], t.pr.at[4 + l, k], p.dev(y=p.yk(k)))

        src = (t.wa, t.wu, t.wd)
        inner = lax.rem((z + 1) // 2, 2)
        mate = z + 1 - 2 * lax.rem(z, 2)
        cross = 2 - z // 2
        holds = (z, mate, cross, 3 - 3 * (z // 2))

        def red(m, k):
            jp, xp, cp = p.cell(k)
            b = src[m].at[jp] if m == 0 else src[m].at[:, blk(jp, TILE)]
            dst = W.at[x * 3 + m, blk(2 * y + c, R), blk(z, TILE)]
            if k == 0:
                return pltpu.make_async_copy(b, dst, t.red_r.at[x * 3 + m, c])
            return rcopy(b, dst, t.red_s.at[m, k], t.red_r.at[x * 3 + m, c], p.dev(x=xp, c=cp))

        def chunk(lm, k):
            return W.at[lm, blk(y, R2), blk(holds[k], TILE)]

        def wz(lm, k):
            b = chunk(lm, 0)
            if k == 1:
                return rcopy(b, b, t.fz_s.at[lm, 0], t.fz_r.at[lm, 1], p.dev(z=mate))
            return rcopy(b, b, t.fz_s.at[lm, 1], t.fz_r.at[lm, 3 - inner], p.dev(z=cross))

        def wrelay(lm, k):
            b = chunk(lm, k)
            return rcopy(b, b, t.fz_s.at[lm, k], t.fz_r.at[lm, k], p.dev(z=mate))

        def wy(lm, k, ky):
            b = chunk(lm, k)
            return rcopy(b, b, t.fy_s.at[lm, k, ky], t.fy_r.at[lm, k, ky], p.dev(y=p.yk(ky)))

        def release(lm):
            for cs in range(2):
                b = W.at[lm, blk(2 * y + cs, R), blk(z, TILE)]
                pltpu.make_async_copy(b, b, t.red_r.at[lm, cs]).wait()
            wz(lm, 2).start()
            wz(lm, 1).start()
            for ky in range(1, Y):
                wy(lm, 0, ky).start()

        def hand_on(lm, k):
            pltpu.make_async_copy(chunk(lm, k), chunk(lm, k), t.fz_r.at[lm, k]).wait()
            if k >= 2:

                @pl.when(inner == 1)
                def _():
                    wrelay(lm, k).start()

            for ky in range(1, Y):
                wy(lm, k, ky).start()
            if k == 3 and lm + 2 < 6:
                release(lm + 2)

        queue = [(lm, k) for lm in range(6) for k in (1, 2, 3)]
        handed = []

        def pump(n=1):
            for _ in range(n):
                if queue:
                    lm, k = queue.pop(0)
                    hand_on(lm, k)
                    handed.append((lm, k))

        def ready(lm, k):
            while k and (lm, k) not in handed:
                pump()
            for ky in range(1, Y):
                wy(lm, k, ky).wait_recv()

        def where(l, m):
            return t.DX if (l, m) == (1, 2) else W.at[3 * l + m]

        def y_part(l, m, k, kz):
            cols = blk(p.zk(kz), TILE)
            return rcopy(
                where(l, m).at[blk(p.yk(k), R2), cols], t.YR.at[m, k - 1, :, cols],
                t.y_s.at[3 * l + m, k, kz], t.y_r.at[3 * l + m, k, kz], p.dev(y=p.yk(k)),
            )

        def z_part(l, m, k):
            return rcopy(
                where(l, m).at[blk(y, R2), blk(p.zk(k), TILE)], t.ZR.at[3 * l + m, k - 1],
                t.z_s.at[3 * l + m, k], t.z_r.at[3 * l + m, k], p.dev(z=p.zk(k)),
            )

        order = (2, 1, 3, 0)

        begun = set()

        def y_start(l, m):
            begun.add((l, m))
            for kz in order:
                for k in range(1, Y):
                    y_part(l, m, k, kz).start()

        def y_sum(l, m, kz):
            cols = blk(p.zk(kz), TILE)
            buf = where(l, m)
            for k in range(1, Y):
                y_part(l, m, k, kz).wait_recv()
            v = buf[blk(y, R2), cols].astype(F32)
            for k in range(1, Y):
                v = v + t.YR[m, k - 1, :, cols].astype(F32)
            buf[blk(y, R2), cols] = v.astype(BF)
            if kz:
                z_part(l, m, kz).start()

        def c_part(l, m, cp):
            lm = 3 * l + m
            return rcopy(t.RD.at[lm, cp], t.CR.at[m, j], t.c_s.at[lm, cp], t.c_r.at[m, j], p.dev(x=l, c=cp))

        def to_owner(l, remote, local):
            for cp in range(2):
                mine = jnp.logical_and(x == l, c == cp)

                @pl.when(mine)
                def _():
                    local(cp).start()

                @pl.when(jnp.logical_not(mine))
                def _():
                    remote(cp).start()

        def z_sum(l, m):
            for k in range(1, nz):
                z_part(l, m, k).wait_recv()
            lm = 3 * l + m
            v = where(l, m)[blk(y, R2), blk(z, TILE)].astype(F32)
            for k in range(1, nz):
                v = v + t.ZR[lm, k - 1].astype(F32)
            t.RD[lm] = v.astype(BF).reshape(2, R, TILE)
            to_owner(
                l, lambda cp: c_part(l, m, cp),
                lambda cp: pltpu.make_async_copy(t.RD.at[lm, cp], t.CR.at[m, j], t.c_r.at[m, j]),
            )

        steps = []
        for n in range(6):
            l, m = 1 - n // 3, 2 - n % 3
            steps += [(y_sum, (l, m, kz)) for kz in order]
            if n:
                steps.append((z_sum, (1 - (n - 1) // 3, 2 - (n - 1) % 3)))
        steps.append((z_sum, (0, 0)))

        def push(n=1):
            for _ in range(n):
                if steps and steps[0][1][:2] in begun:
                    f, a = steps.pop(0)
                    f(*a)

        def push_through(f, l, m):
            while any(g is f and a[:2] == (l, m) for g, a in steps):
                push()

        def s_y(l, k):
            return rcopy(t.SG.at[l], t.SYR.at[l, k - 1], t.sy_s.at[l, k], t.sy_r.at[l, k], p.dev(y=p.yk(k)))

        def s_z(l, k):
            return rcopy(t.SRD.at[l], t.SZR.at[l, k - 1], t.sz_s.at[l, k], t.sz_r.at[l, k], p.dev(z=p.zk(k)))

        def s_c(l, cp):
            return rcopy(t.SRD.at[2 + l], t.SCR.at[j], t.sc_s.at[l, cp], t.sc_r.at[j], p.dev(x=l, c=cp))

        def s_start(l):
            for k in range(1, Y):
                s_y(l, k).start()

        def s_mid(l):
            for k in range(1, Y):
                s_y(l, k).wait_recv()
            t.SRD[l] = t.SG[l] + jnp.sum(t.SYR[l], axis=0)
            for k in range(1, nz):
                s_z(l, k).start()

        def s_end(l):
            for k in range(1, nz):
                s_z(l, k).wait_recv()
            t.SRD[2 + l] = t.SRD[l] + jnp.sum(t.SZR[l], axis=0)
            to_owner(
                l, lambda cp: s_c(l, cp), lambda cp: pltpu.make_async_copy(t.SRD.at[2 + l], t.SCR.at[j], t.sc_r.at[j])
            )

        kept = list(spilled)

        def save(name):
            i = kept.index(name)
            return pltpu.make_async_copy(getattr(t, name), getattr(t, "o_" + name), t.keep.at[0, i])

        def fetch(name):
            i = kept.index(name)
            return pltpu.make_async_copy(getattr(t, "o_" + name), getattr(t, name), t.keep.at[1, i])

        def add_small(l, r, v):
            t.SG[l, pl.ds(r, 1), :] += v

        def put_small(l, r, acc):
            v = jnp.sum(acc, axis=0, keepdims=True)
            for q in range(4):
                add_small(l, 4 * r + q, v[:, q * TILE : (q + 1) * TILE])

        def own_rows(g, r):
            return pl.ds(pl.multiple_of((2 * g + x) * RP + r * RC, RC), RC)

        def attend(l, g, zz):
            rows_, cols = half(g), blk(zz, TILE)
            v = mm(t.NF[rows_, :], W[3 * l, :, cols], NN)
            t.PR[rows_, cols] = (v + t.SPS[l, pl.ds(24 + zz, 1), :]).astype(BF)
            live = lax.broadcasted_iota(jnp.int32, (RP, RP), 1) < SEQ
            for i in range(2):
                im = 2 * g + i
                b = t.PR[row(g, i), cols]
                q, k, v = b[:, 0:HD], b[:, HD : 2 * HD], b[:, 2 * HD : 3 * HD]
                s = jnp.where(live, mm(q, k, NT) * SCALE, -1e30)
                w = jnp.exp(s - jnp.max(s, axis=-1, keepdims=True))
                pb = (w * (1.0 / jnp.sum(w, axis=-1, keepdims=True))).astype(BF)
                t.PB[4 * im + zz] = pb
                o = mm(pb, v, NN).astype(BF)
                t.MX[row(g, i), cols] = jnp.concatenate([jnp.zeros((RP, 3 * HD), BF), o], axis=1)
                t.PR[row(g, i), cols] = jnp.concatenate([b[:, : 3 * HD], o], axis=1)

        def project(lhs, lm, g):
            rows_ = half(g)

            def step(n, _):
                cols = blk(n, TILE)
                OP[rows_, cols] = mm(lhs[rows_, :], W[lm, cols, :], NT).astype(BF)
                return 0

            lax.fori_loop(0, 4, step, 0)

        def up(l, g, zz):
            rows_, cols = half(g), blk(zz, TILE)
            u = mm(t.N2[rows_, :], W[3 * l + 1, :, cols], NN) + t.SPS[l, pl.ds(28 + zz, 1), :]
            cdf = 0.5 + 0.5 * lax.erf(u * (1.0 / math.sqrt(2.0)))
            t.H[rows_, cols] = (u * cdf).astype(BF)
            t.GD[rows_, cols] = (cdf + u * jnp.exp(-0.5 * u * u) * (1.0 / math.sqrt(2.0 * math.pi))).astype(BF)

        def pre(l, g):
            rows_ = half(g)

            def step(n, _):
                cols = blk(n, TILE)
                v = mm(t.GT[rows_, :], W[3 * l + 2, :, cols], NN) * t.GD[rows_, cols].astype(F32)
                gp = v.astype(BF)
                t.GD[rows_, cols] = gp
                add_small(l, 28 + n, jnp.sum(gp.astype(F32), axis=0, keepdims=True))
                return 0

            lax.fori_loop(0, 4, step, 0)

        def weight_grad(buf, pairs):
            def step(r, _):
                cols = blk(r, TILE)
                v = mm(pairs[0][0][:, cols], pairs[0][1][...], TN)
                for a, b in pairs[1:]:
                    v = v + mm(a[:, cols], b[...], TN)
                buf[cols, :] = v.astype(BF)
                return 0

            lax.fori_loop(0, 4, step, 0)

        def attend_back(l, g):
            rows_ = half(g)

            def mixed(n, _):
                cols = blk(n, TILE)
                t.H[rows_, cols] = mm(t.MX[rows_, :], W[3 * l, :, cols], NN).astype(BF)
                return 0

            lax.fori_loop(0, 4, mixed, 0)

            def step(i, _):
                im = 2 * g + i
                ri = blk(im, RP)
                for zz in range(4):
                    cols = blk(zz, TILE)
                    b = t.PR[ri, cols]
                    q, k, v = b[:, 0:HD], b[:, HD : 2 * HD], b[:, 2 * HD : 3 * HD]
                    gm = t.H[ri, cols][:, 3 * HD : 4 * HD]
                    pb = t.PB[4 * im + zz]
                    pf = pb.astype(F32)
                    gp = mm(gm, v, NT)
                    cen = jnp.sum(pf * gp, axis=-1, keepdims=True)
                    gsc = (pf * (gp - cen)).astype(BF)
                    gq = mm(gsc, k, NN) * SCALE
                    gk = mm(gsc, q, TN) * SCALE
                    gv = mm(pb, gm, TN)
                    out = jnp.concatenate([gq, gk, gv, jnp.zeros((RP, HD), F32)], axis=1).astype(BF)
                    t.H[ri, cols] = out
                    t.PR[ri, cols] = jnp.concatenate([jnp.zeros((RP, 3 * HD), BF), b[:, 3 * HD :]], axis=1)
                    add_small(l, 24 + zz, jnp.sum(out.astype(F32), axis=0, keepdims=True))
                return 0

            lax.fori_loop(0, 2, step, 0)

        def rows_loop(step, init=0):
            return lax.fori_loop(0, RP // RC, step, init)

        t.XO[...] = jnp.zeros((2, RP, D), BF)
        t.GT[...] = jnp.zeros(full, BF)
        for m in range(2):
            t.XO[m, 0:SEQ, :] = t.img[m]
            t.GT[pl.ds(pl.multiple_of((2 * c + m) * RP, RC), SEQ), :] = t.cot[m]
        t.SG[...] = jnp.zeros((2, 32, TILE), F32)
        p.barrier()
        for k in range(4):
            small_red(k).start()
        for m in range(3):
            for k in (1, 2, 3, 0):
                red(m, k).start()
        for l in range(2):
            for cs in range(2):
                b = t.SPB.at[l, y, z, cs]
                pltpu.make_async_copy(b, b, t.pr.at[l, cs]).wait()
            for k in range(1, nz):
                small_z(l, k).start()
        release(0)
        for l in range(2):
            for k in range(1, nz):
                small_z(l, k).wait_recv()
            for k in range(1, Y):
                small_y(l, k).start()
        for l in range(2):
            for k in range(1, Y):
                small_y(l, k).wait_recv()
            t.SPS[l] = jnp.sum(t.SPB[l].astype(F32).reshape(Y * nz * 2, 32, TILE), axis=0)
            for r in range(6):
                for q in range(4):
                    t.G[l, r : r + 1, q * TILE : (q + 1) * TILE] = t.SPS[l, 4 * r + q : 4 * r + q + 1, :]

        def ln(l, g, b, load, buf, at):
            gain, shift = t.G[l, g : g + 1, :], t.G[l, b : b + 1, :]

            def step(r, _):
                buf[at(r), :] = norm_row(load(r), gain, shift).astype(BF)
                return 0

            rows_loop(step)

        for m in range(2):
            ln(
                0, 0, 2, lambda r, m=m: t.XO[m, blk(r, RC), :].astype(F32), t.NF,
                lambda r, m=m: pl.ds(pl.multiple_of((2 * c + m) * RP + r * RC, RC), RC),
            )
        first = ag_local(t.NF, 0)
        for cp in first:
            cp.start()
        tops = ag_local(t.GT, 4)
        for cp in tops:
            cp.start()
        release(1)
        pump(1)
        for cp in first:
            cp.wait_recv()

        for l in range(2):
            A, U, DN = 3 * l, 3 * l + 1, 3 * l + 2
            s = 2 * l
            if l:
                ag_in(t.NF, 0, 2)
            for k in range(4):
                ready(A, k)
                attend(l, 0, holds[k])
                if l == 0 or k < 2:
                    pump()
            if l:
                rs_done(0, 1)
                rs_done(1, 1)
            project(t.MX, A, 0)
            rs_out(0, s)
            if l:
                ag_mid(t.NF, 1, 2)
                ag_in(t.NF, 1, 2)
            for k in range(4):
                attend(l, 1, holds[k])
                if k % 2:
                    pump()
            project(t.MX, A, 1)
            rs_out(1, s)
            if l == 0:
                for cp in first:
                    cp.wait_send()
                for name in ("NF", "PR", "PB"):
                    save(name).start()
            else:
                ag_done(t.NF, 2)

            def second(g):
                gain, shift, bias = t.G[l, 1:2, :], t.G[l, 4:5, :], t.G[l, 3:4, :]

                def step(r, _):
                    rs = blk(r, RC)
                    v = t.XO[x, rs, :] if l == 0 else t.OUT[0, rs, :]
                    mid = v.astype(F32) + sums(g, r) + bias
                    t.MID[l, rs, :] = mid
                    t.N2[own_rows(g, r), :] = norm_row(mid, gain, shift).astype(BF)
                    return 0

                rows_loop(step)
                ag_send(t.N2, g, 1 + 2 * l)

            pump()
            for g in range(2):
                rs_in(g, s, lambda g=g: second(g))
            pump()
            ag_mid(t.N2, 0, 1 + 2 * l)
            ag_in(t.N2, 0, 1 + 2 * l)
            if l:
                save("H").wait()
                save("GD").wait()
            for k in range(4):
                ready(U, k)
                up(l, 0, holds[k])
            ag_mid(t.N2, 1, 1 + 2 * l)
            pump()
            ag_in(t.N2, 1, 1 + 2 * l)
            for k in range(4):
                up(l, 1, holds[k])
            pump()
            ag_done(t.N2, 1 + 2 * l)
            rs_done(0, s)
            rs_done(1, s)
            if l == 0:
                for name in ("N2", "H", "GD"):
                    save(name).start()
                for name in ("NF", "PR", "PB"):
                    save(name).wait()
            else:
                for cp in tops:
                    cp.wait_recv()
                weight_grad(t.DX, [(t.GT, t.H)])
                y_start(1, 2)
            for k in range(4):
                ready(DN, k)
            s = 2 * l + 1
            project(t.H, DN, 0)
            rs_out(0, s)
            pump()
            project(t.H, DN, 1)
            rs_out(1, s)
            pump()
            if l == 0:
                save("N2").wait()

                def last(g):
                    gain, shift, bias = t.G[1, 0:1, :], t.G[1, 2:3, :], t.G[0, 5:6, :]

                    def step(r, _):
                        rs = blk(r, RC)
                        o = (t.MID[0, rs, :] + sums(g, r) + bias).astype(BF)
                        t.OUT[0, rs, :] = o
                        t.NF[own_rows(g, r), :] = norm_row(o.astype(F32), gain, shift).astype(BF)
                        return 0

                    rows_loop(step)
                    ag_send(t.NF, g, 2)

                for g in range(2):
                    rs_in(g, s, lambda g=g: last(g))
                pump()
                ag_mid(t.NF, 0, 2)

                @pl.when(x != 0)
                def _():
                    rcopy(t.OUT.at[0], t.LOB, t.lo_s.at[0], t.lo_r.at[0], p.dev(x=1 - x)).start()
            else:
                for g in range(2):

                    @pl.when(c == g)
                    def _():
                        def step(r, _):
                            rs = blk(r, RC)
                            t.GMID[rs, :] = t.MID[1, rs, :] + OP[own_rows(g, r), :].astype(F32) + t.G[1, 5:6, :]
                            return 0

                        rows_loop(step)

        for k in range(1, 4):
            small_red(k).wait_send()
        for l in range(2):
            for k in range(1, nz):
                small_z(l, k).wait_send()
            for k in range(1, Y):
                small_y(l, k).wait_send()
        for m in range(3):
            for k in range(1, 4):
                red(m, k).wait_send()
        for lm in range(6):
            wz(lm, 1).wait_send()
            wz(lm, 2).wait_send()
            for k in (2, 3):

                @pl.when(inner == 1)
                def _():
                    wrelay(lm, k).wait_send()

            for k in range(4):
                for ky in range(1, Y):
                    wy(lm, k, ky).wait_send()

        def final_out(g):
            def step(r, _):
                rs = blk(r, RC)
                v = t.GMID[rs, :] + RB[1, x, rs, :].astype(F32) + XR[1, rs, :].astype(F32)
                t.OUT[1, rs, :] = v.astype(BF)
                return 0

            rows_loop(step)

        zero8 = jnp.zeros((8, D), F32)
        for l in (1, 0):
            A, U, DN = 3 * l, 3 * l + 1, 3 * l + 2
            s = 4 + 2 * (1 - l)
            if l == 0:
                ag_in(t.GT, 0, 6)
                fetch("GD").wait()
            rs_done(0, s - 1)
            rs_done(1, s - 1)
            pre(l, 0)
            project(t.GD, U, 0)
            rs_out(0, s)
            push()
            if l == 0:
                ag_mid(t.GT, 1, 6)
                ag_in(t.GT, 1, 6)
            pre(l, 1)
            project(t.GD, U, 1)
            rs_out(1, s)
            push()
            if l == 1:
                for cp in tops:
                    cp.wait_send()
                weight_grad(W.at[U], [(t.N2, t.GD)])
                y_start(1, 1)
                fetch("N2").start()
                fetch("GD").start()
                for g in range(2):
                    rs_in(g, 3, lambda g=g: final_out(g))
                push()

                @pl.when(x != 1)
                def _():
                    rcopy(t.OUT.at[1], t.LOB, t.lo_s.at[0], t.lo_r.at[0], p.dev(x=1 - x)).start()
            else:
                ag_done(t.GT, 6)
                fetch("H").wait()
                push_through(y_sum, 1, 0)
                weight_grad(W.at[DN], [(t.GT, t.H)])
                y_start(0, 2)

            def mid_back(g):
                def step(r, acc):
                    rs = blk(r, RC)
                    dy = sums(g, r)
                    top = t.GT[own_rows(g, r), :].astype(F32)
                    dx, dg = norm_back(t.MID[l, rs, :], t.G[l, 1:2, :], dy)
                    gmid = top + dx
                    t.GMID[rs, :] = gmid
                    t.MX[own_rows(g, r), :] = gmid.astype(BF)
                    return acc[0] + fold(dg), acc[1] + fold(dy), acc[2] + fold(gmid), acc[3] + fold(top)

                acc = rows_loop(step, (zero8,) * 4)
                put_small(l, 1, acc[0])
                put_small(l, 4, acc[1])
                put_small(l, 3, acc[2])
                put_small(l, 5, acc[3])
                ag_send(t.MX, g, s + 1)

            for g in range(2):
                rs_in(g, s, lambda g=g: mid_back(g))
            push()
            if l == 0:
                fetch("N2").wait()
                weight_grad(W.at[U], [(t.N2, t.GD)])
                y_start(0, 1)
                for name in ("PR", "PB"):
                    fetch(name).wait()
            ag_mid(t.MX, 0, s + 1)
            ag_in(t.MX, 0, s + 1)
            push()
            attend_back(l, 0)
            push()
            rs_done(0, s)
            rs_done(1, s)
            project(t.H, A, 0)
            rs_out(0, s + 1)
            push()
            ag_mid(t.MX, 1, s + 1)
            ag_in(t.MX, 1, s + 1)
            attend_back(l, 1)
            push()
            project(t.H, A, 1)
            rs_out(1, s + 1)
            ag_done(t.MX, s + 1)
            if l == 1:
                push_through(y_sum, 1, 1)
            else:
                fetch("NF").wait()
                push_through(y_sum, 0, 2)
            weight_grad(W.at[A], [(t.NF, t.H), (t.MX, t.PR)])
            y_start(l, 0)
            if l == 1:
                for name in ("H", "PR", "PB", "NF"):
                    fetch(name).start()

            def first_back(g):
                def step(r, acc):
                    rs = blk(r, RC)
                    dy = sums(g, r)
                    v = (t.XO[x, rs, :] if l == 0 else t.OUT[0, rs, :]).astype(F32)
                    dx, dg = norm_back(v, t.G[l, 0:1, :], dy)
                    gx = (t.GMID[rs, :] + dx).astype(BF)
                    t.IGB[l, rs, :] = gx
                    if l == 1:
                        t.GT[own_rows(g, r), :] = gx
                    return acc[0] + fold(dg), acc[1] + fold(dy)

                acc = rows_loop(step, (zero8,) * 2)
                put_small(l, 0, acc[0])
                put_small(l, 2, acc[1])
                if l == 1:
                    ag_send(t.GT, g, 6)

            for g in range(2):
                rs_in(g, s + 1, lambda g=g: first_back(g))
            s_start(l)

            @pl.when(x != l)
            def _():
                rcopy(t.IGB.at[l], t.LGB, t.lo_s.at[1], t.lo_r.at[1], p.dev(x=1 - x)).start()

            if l == 1:
                ag_mid(t.GT, 0, 6)
                s_mid(1)

        s_end(1)
        push(3)
        s_mid(0)
        push(100)
        s_end(0)
        for i, (buf, got, out) in enumerate(((t.OUT, t.LOB, t.lo), (t.IGB, t.LGB, t.ig))):
            cp = rcopy(buf.at[x], got, t.lo_s.at[i], t.lo_r.at[i], p.dev(x=1 - x))
            cp.wait_recv()
            cp.wait_send()
            out[x] = buf[x, 0:SEQ, :]
            out[1 - x] = got[0:SEQ, :]
        for m in (2, 1, 0):
            for jj in range(4):
                b = t.CR.at[m, jj]
                pltpu.make_async_copy(b, b, t.c_r.at[m, jj]).wait()
                v = t.CR[m, jj].astype(F32)
                if m == 0:
                    t.ga[jj] = v
                elif m == 1:
                    t.gu[:, jj * TILE : (jj + 1) * TILE] = v
                else:
                    t.gd[:, jj * TILE : (jj + 1) * TILE] = v
        for jj in range(4):
            b = t.SCR.at[jj]
            pltpu.make_async_copy(b, b, t.sc_r.at[jj]).wait()
            t.gs_out[jj] = t.SCR[jj]
        for g in range(2):
            rs_done(g, 7)
        for l in range(2):
            for m in range(3):
                for kz in range(nz):
                    for k in range(1, Y):
                        y_part(l, m, k, kz).wait_send()
                    if kz:
                        z_part(l, m, kz).wait_send()
            for k in range(1, Y):
                s_y(l, k).wait_send()
            for k in range(1, nz):
                s_z(l, k).wait_send()
            for cp in range(2):

                @pl.when(jnp.logical_not(jnp.logical_and(x == l, c == cp)))
                def _():
                    s_c(l, cp).wait_send()
                    for m in range(3):
                        c_part(l, m, cp).wait_send()

    vm = pl.BlockSpec(memory_space=pltpu.VMEM)
    hbm = pl.BlockSpec(memory_space=pl.ANY)
    return pl.pallas_call(
        body,
        out_shape=[jax.ShapeDtypeStruct(*a) for a in outputs.values()]
        + [jax.ShapeDtypeStruct(a, BF) for a in spilled.values()],
        in_specs=[vm, vm] + [hbm] * 4,
        out_specs=[vm] * len(outputs) + [hbm] * len(spilled),
        scratch_shapes=[pltpu.VMEM(*a) for a in vmem.values()] + [dma(a) for a in sems.values()],
        compiler_params=pltpu.CompilerParams(
            collective_id=0, has_side_effects=True, vmem_limit_bytes=VMEM_LIMIT
        ),
    )


def small_pack(norm_gains, row_shifts, head_bias, unit_bias, dpn, nz):
    dp, z = lax.axis_index("dp"), lax.axis_index("tensor")
    rows = jnp.concatenate([norm_gains[0], row_shifts[0]], axis=0)
    w = rows.shape[1]
    rows = lax.dynamic_update_slice(jnp.zeros((6, D), BF), rows, (0, (dp * nz + z) * w)).reshape(1, 24, TILE)
    hw, uw = head_bias.shape[3], unit_bias.shape[2]
    head = jnp.zeros((4, 4, TILE), BF)
    head = lax.dynamic_update_slice(head, head_bias[0, 0][:, None], (0, z, dp * hw))
    head = lax.dynamic_update_slice(head, head_bias[0, 1][:, None], (0, z, 2 * HD + dp * hw))
    unit = lax.dynamic_update_slice(jnp.zeros((4, 4, TILE), BF), unit_bias[0][:, None], (0, z, dp * uw))
    return jnp.concatenate([jnp.broadcast_to(rows, (4, 24, TILE)), head, unit], axis=1)


def solution(mesh):
    dpn, nz = mesh.shape["dp"], mesh.shape["tensor"]

    def on_device(
        images_in, cotangent, w_qkv, w_out, w_up, w_down, norm_gains, row_shifts, head_bias, unit_bias
    ):
        R = w_up.shape[1]
        qkv = w_qkv[0].reshape(R, 3, 4, HD).transpose(2, 0, 1, 3).reshape(4, R, 3 * HD)
        wo = w_out[0].reshape(R, 4, HD).transpose(1, 0, 2)
        wa = jnp.concatenate([qkv, wo], axis=2)
        sp = small_pack(norm_gains, row_shifts, head_bias, unit_bias, dpn, nz)
        lo, ig, ga, gu, gd, gs = both_layers(dpn, nz, R)(images_in, cotangent, wa, w_up[0], w_down[0], sp)[:6]
        dp, z = lax.axis_index("dp"), lax.axis_index("tensor")
        g_qkv = ga[:, :, : 3 * HD].reshape(4, R, 3, HD).transpose(1, 2, 0, 3).reshape(w_qkv.shape)
        g_out = ga[:, :, 3 * HD :].transpose(1, 0, 2).reshape(w_out.shape)
        w, hw, uw = norm_gains.shape[2], head_bias.shape[3], unit_bias.shape[2]
        rows = lax.dynamic_slice(jnp.sum(gs[:, :24], axis=0).reshape(6, D), (0, (dp * nz + z) * w), (6, w))
        head = lax.dynamic_slice(gs, (0, 24 + z, 0), (4, 1, TILE))[:, 0]
        unit = lax.dynamic_slice(gs, (0, 28 + z, dp * uw), (4, 1, uw))[:, 0]
        g_head = jnp.stack([lax.dynamic_slice(head, (0, o + dp * hw), (4, hw)) for o in (0, 2 * HD)])
        return (
            lo[None], ig[None], g_qkv, g_out, gu[None], gd[None],
            rows[None, :2], rows[None, 2:], g_head[None], unit[None],
        )

    in_specs = (
        P(None, ("dp", "tensor"), None),
        P(None, ("dp", "tensor"), None),
        P("section", "dp", None, "tensor"),
        P("section", "dp", "tensor"),
        P("section", "dp", "tensor"),
        P("section", "dp", "tensor"),
        P("section", None, ("dp", "tensor")),
        P("section", None, ("dp", "tensor")),
        P("section", None, "tensor", "dp"),
        P("section", "tensor", "dp"),
    )
    out_specs = (
        P("section", None, ("dp", "tensor"), None),
        P("section", None, ("dp", "tensor"), None),
        P("section", "dp", None, "tensor"),
        P("section", "dp", "tensor"),
        P("section", "dp", "tensor"),
        P("section", "dp", "tensor"),
        P("section", None, ("dp", "tensor")),
        P("section", None, ("dp", "tensor")),
        P("section", None, "tensor", "dp"),
        P("section", "tensor", "dp"),
    )
    return jax.shard_map(
        on_device, mesh=mesh, in_specs=in_specs, out_specs=out_specs, check_vma=False
    )
```

time: 1740 us -> 427 us (0.25)
  waiting for transfers between devices: 587 us -> 0 us
  blocking collectives: 496 us -> 0 us
  Pallas kernels: 0 us -> 393 us
  matrix products: 259 us -> 0 us
  local copies, waits for them, and re-layouts: 251 us -> 21.1 us
  other arithmetic: 76.1 us -> 2.91 us
  starting transfers between devices: 38.9 us -> 0 us
    unnamed x10 -> x0, blocking collectives: 408 us -> none
    pallas_call x0 -> x1, Pallas kernels: none -> 393 us  [on_device(): both_layers(dpn, nz, R)(images_in, cotangent, wa, w_up[0], w_down[0], sp)]
    all_gather x15 -> x0, waiting for transfers between devices: 343 us -> none  [the longest x6 156 us: spread_grads(): return lax.all_gather(local_rows, 'tensor', axis=0, tiled=True)]
    dot_general x120 -> x0, matrix products: 259 us -> none  [the longest x12 41.5 us: partial_term(): lax.dot_general(left_rows, right_side, LAST_CONTRACT, preferred_element_t...]
    reduce_scatter x4 -> x0, waiting for transfers between devices: 117 us -> none  [the longest x1 32.5 us: reduce_grads(): lax.psum_scatter(weight_grads[3].astype(jnp.bfloat16), 'dp', scatter_dime...]
    unnamed x39 -> x0, waiting for transfers between devices: 96 us -> none
    unnamed x249 -> x26, local copies, waits for them, and re-layouts: 106 us -> 12.1 us
    all_gather x5 -> x0, blocking collectives: 88.1 us -> none  [the longest x1 36.1 us: on_device(): lax.all_gather(row_shifts[0], ('dp', 'tensor'), axis=1, tiled=True)]
  transfers between devices with their start and end apart: 39 -> 0, of which waited for: 32 -> 0; matrix products, arithmetic and copies ran while one was open for 27% -> 0% of each run, Pallas kernels for 0% -> 0%
where the time goes in v2:
time: 427 us; the launch traced here: 418 us
  Pallas kernels  393 us (92%)
  local copies, waits for them, and re-layouts  21.1 us (5%)
    pallas_call x1, Pallas kernels, on_device(): both_layers(dpn, nz, R)(images_in, cotangent, wa, w_up[0], w_down[0], sp)  393 us
    unnamed x26, local copies, waits for them, and re-layouts  12.1 us

profile of v2, /device:TPU:21, one launch (start us, length us, event | category | flops | bytes accessed | tf_op | source)
XLA Modules:
  0.0 418.5 jit_solution(14244326162886617279)
XLA Ops:
  0.6 0.0 copy-start.6
  0.7 0.7 slice_bitcast_fusion.3
  1.4 0.8 dynamic_update_slice.13
  2.2 0.7 dynamic_update_slice.14
  2.9 0.7 copy.35
  3.6 0.7 dynamic_update_slice.15
  4.4 0.7 pad_maximum_fusion.2
  5.1 0.1 dynamic_update_slice.12
  5.3 0.6 pad_maximum_fusion.1.refs_5_
  5.9 1.2 copy.28
  7.1 0.0 copy-start.4
  7.1 0.2 copy.32
  7.3 0.0 copy-done.6
  7.4 0.1 copy.30
  7.5 0.0 copy-start.5
  7.5 0.2 copy.31
  7.6 1.0 pad_maximum_fusion.refs_2_
  8.6 0.0 copy-done.4
  8.6 1.1 copy.36.refs_0_
  9.7 0.0 copy-done.5
  9.7 1.1 copy.37.refs_1_
  10.8 393.2 %shard_map.177 = (bf16[2,197,1024]{2,1,0:T(8,128)(2,1)}, bf16[2,197,1024]{2,1,0:T(8,128)(2,1)}, f32[4,256,256]{2,1,0:T(8,128)}, f32[256,1024]{1,0:T(8,128)}, f32...) custom-call(bf16[2,197,1024]{2,1,0:T(8,128)(2,1)} %copy.36.refs_0_, ...), custom_call_target="tpu_custom_call" | custom-call | tf_op jit(solution)/shard_map/pallas_call | solution.py:964
  404.0 0.9 constant_dynamic-slice_fusion.2
  404.9 0.6 maximum_bitcast_fusion
  405.5 1.5 copy.38
  407.0 0.0 copy-start
  407.1 0.1 copy.39
  407.1 1.1 copy.43
  408.3 0.0 copy-done
  408.3 0.2 slice_bitcast_fusion
  408.5 0.0 copy-start.3
  408.5 0.2 copy.40
  408.7 0.8 copy.44
  409.5 0.0 copy-start.7
  409.5 0.0 copy-start.2
  409.5 3.0 copy.41
  412.5 0.0 copy-done.3
  412.5 0.0 copy-start.1
  412.5 1.7 copy.42
  414.2 0.0 copy-done.7
  414.2 0.1 constant_dynamic-slice_fusion.3
  414.3 0.6 slice_bitcast_fusion.1
  414.9 0.6 slice_bitcast_fusion.2
  415.4 0.7 constant_dynamic-slice_fusion
  416.1 0.0 copy-done.2
  416.1 1.0 copy.51
  417.1 0.0 copy-done.1
  417.1 1.0 copy.52
  (10 shorter events, 0.1 us)
Async XLA Ops:
  0.6 6.7 %copy-start.6 = (bf16[1,256,256]{2,1,0:T(8,128)(2,1)S(1)}, bf16[1,256,256]{2,1,0:T(8,128)(2,1)}, u32[]{:S(2)}) copy-start(bf16[1,256,256]{2,1,0:T(8,128)(2,1)} %param.13) | copy-start | bytes 393220
  7.1 1.5 copy-start.4
  7.5 2.3 copy-start.5
  407.0 1.2 copy-start
  408.5 4.0 copy-start.3
  409.5 4.7 %copy-start.7 = (f32[4,32,256]{2,1,0:T(8,128)S(1)}, f32[4,32,256]{2,1,0:T(8,128)}, u32[]{:S(2)}) copy-start(f32[4,32,256]{2,1,0:T(8,128)} %get-tuple-element.21) | copy-start | bytes 393220
  409.5 6.6 %copy-start.2 = (f32[256,1024]{1,0:T(8,128)S(1)}, f32[256,1024]{1,0:T(8,128)}, u32[]{:S(2)}) copy-start(f32[256,1024]{1,0:T(8,128)} %get-tuple-element.19) | copy-start | bytes 3145732
  412.5 4.6 %copy-start.1 = (f32[256,1024]{1,0:T(8,128)S(1)}, f32[256,1024]{1,0:T(8,128)}, u32[]{:S(2)}) copy-start(f32[256,1024]{1,0:T(8,128)} %get-tuple-element.20) | copy-start | bytes 3145732
